TPU v7x, 32 devices: a whole 2x2x4 slice. The times are simulated.
32 devices in a mesh: group: 2 (over x), tile: 16 (over z, y, core).
Axes of the slice: x: 2, y: 2, z: 4, core: 2. Of those that a mesh axis runs over, the one named last changes fastest.
Arguments:
- tracer: float32 [32, 15, 384, 128], P('group', None, 'tile'), parts along dimension 0, may hold values from 0.01 to 9
- courant_frac: float32 [32, 384, 128], P('group', 'tile'), parts along dimension 0, may hold values from 0.05 to 0.95
- departure_shift: int32 [32, 128], P('group'), parts along dimension 0, may hold values from 0 to 2, as said below
- cell_area: float32 [384, 128], P('tile'), may hold values from 0.6 to 1.6
- adjoint_seed: float32 [32, 15, 384, 128], P('group', None, 'tile'), parts along dimension 0, may hold values from -4 to 6
Outputs:
- tracer_next: float32 [32, 15, 384, 128], P('group', None, 'tile'), parts along dimension 0
- tracer_adjoint: float32 [32, 15, 384, 128], P('group', None, 'tile'), parts along dimension 0
There are 2 independent parts, one for each index of `group`. A program takes and returns all parts, laid end to end along the dimension named above; an argument that names none is the same for every part. Nothing has to cross between parts.
Inputs may be any that keep to these rules, and one draw needn't show every extreme that they name: `departure_shift`: the largest offset is reached in every draw.
All inputs are finite; a program needn't handle non-finite values.
Results may differ from a plain program's by a relative error of at most 0.00002.
Values sent between devices are 32-bit elements; how exact they have to be, the bound alone decides.
No kernel may reach another device: no remote copies, remote signals or barrier semaphores. Data moves between devices by JAX's collectives and lax.ppermute only.
A program may use at most 128 MiB of HBM per device.

v0:
```python
import jax
import jax.numpy as jnp
from jax import lax
from jax.sharding import PartitionSpec as P

MAXOFF = 2


smooth_floor = 0.1


def extended_2(block, sides, width):
    for axis, dim in sides:
        count = lax.axis_size(axis)
        forward = [(i, i + 1) for i in range(count - 1)]
        forward.append((count - 1, 0))
        backward = [(target, source) for source, target in forward]
        low = lax.ppermute(
            lax.slice_in_dim(block, block.shape[dim] - width, None, axis=dim), axis, forward
        )
        high = lax.ppermute(lax.slice_in_dim(block, 0, width, axis=dim), axis, backward)
        block = jnp.concatenate([low, block, high], axis=dim)
    return block


def advect(window, face_frac, shifts, area_cells, first, cell_count):
    face_count = cell_count + 1
    fracs = face_frac[:, first - 1 : first - 1 + face_count, :][:, None]
    chosen = shifts[:, None, None, :]

    def take_faces(position):
        return window[:, :, position : position + face_count, :]

    fluxes = jnp.zeros_like(take_faces(first - 1))
    carried = jnp.zeros_like(fluxes)
    for shift_count in range(MAXOFF + 1):
        anchor = first - 1 - shift_count
        minus_two = take_faces(anchor - 2)
        minus_one = take_faces(anchor - 1)
        center = take_faces(anchor)
        plus_one = take_faces(anchor + 1)
        plus_two = take_faces(anchor + 2)
        right_edge = 7.0 / 12.0 * (center + plus_one) - 1.0 / 12.0 * (minus_one + plus_two)
        left_edge = 7.0 / 12.0 * (minus_one + center) - 1.0 / 12.0 * (minus_two + plus_one)
        curvature = 6.0 * center - 3.0 * (left_edge + right_edge)
        partial_flux = fracs * (
            right_edge
            - 0.5 * fracs * (right_edge - left_edge - (1.0 - 2.0 * fracs / 3.0) * curvature)
        )
        fluxes = fluxes + jnp.where(chosen == shift_count, carried + partial_flux, 0.0)
        carried = carried + center
    interior = window[:, :, first : first + cell_count, :]
    return interior - (fluxes[:, :, 1:] - fluxes[:, :, :-1]) / area_cells


def shards(tracer, courant_frac, departure_shift, cell_area, adjoint_seed):
    margin = MAXOFF + 3
    bin_count = tracer.shape[1]
    columns = tracer.shape[2]
    stacked = jnp.concatenate([tracer, courant_frac[:, None]], axis=1)
    extended = extended_2(stacked, (("tile", 2),), margin)
    window = extended[:, :bin_count]
    face_frac = extended[:, bin_count]

    def advance(values):
        return advect(values, face_frac, departure_shift, cell_area, margin, columns)

    advected, pullback = jax.vjp(advance, window)
    positive = jnp.sqrt(advected * advected + smooth_floor * smooth_floor)
    mass_before, mass_after, seed_dot = lax.psum(
        (
            jnp.sum(cell_area * tracer, axis=(2, 3)),
            jnp.sum(cell_area * positive, axis=(2, 3)),
            jnp.sum(adjoint_seed * positive, axis=(2, 3)),
        ),
        "tile",
    )
    rescale = (mass_before / mass_after)[:, :, None, None]
    feedback = (mass_before * seed_dot / (mass_after * mass_after))[:, :, None, None]
    direct = cell_area * (seed_dot / mass_after)[:, :, None, None]
    tracer_next = positive * rescale
    seed_second = rescale * adjoint_seed - cell_area * feedback
    seed_first = seed_second * advected / positive
    (gradient,) = pullback(seed_first)
    filler = jnp.zeros(gradient.shape[:2] + (columns - 2 * margin, gradient.shape[3]), jnp.float32)
    outgoing = jnp.concatenate(
        [gradient[:, :, :margin], filler, gradient[:, :, columns + margin :]], axis=2
    )
    incoming = extended_2(outgoing, (("tile", 2),), margin)
    returned = jnp.concatenate(
        [incoming[:, :, :margin], filler, incoming[:, :, columns + margin :]], axis=2
    )
    tracer_adjoint = gradient[:, :, margin : margin + columns] + returned + direct
    return (tracer_next, tracer_adjoint)


def solution(mesh):
    return jax.shard_map(
        shards,
        mesh=mesh,
        in_specs=(
            P("group", None, "tile", None),
            P("group", "tile", None),
            P("group", None),
            P("tile", None),
            P("group", None, "tile", None),
        ),
        out_specs=(P("group", None, "tile", None), P("group", None, "tile", None)),
        check_vma=False,
    )
```

profile of v0, /device:TPU:0, one launch (start us, length us, event | category | flops | bytes accessed | tf_op | source)
XLA Modules:
  0.0 148.6 jit_solution(12652019000116986354)
XLA Ops:
  0.6 1.0 copy.39
  1.6 2.3 %copy.26 = f32[16,15,24,128]{3,0,2,1:T(8,128)S(1)} copy(f32[16,15,24,128]{3,2,1,0:T(8,128)} %param.5) | data formatting | bytes 5898240 | tf_op args[0]
  3.9 0.0 copy-start.6
  4.0 0.1 pad_maximum_fusion.1
  4.1 0.2 copy.21
  4.3 5.5 %collective-permute-start.1 = (f32[16,16,5,128]{3,1,2,0:T(8,128)S(1)}, f32[16,16,5,128]{3,1,2,0:T(8,128)S(1)}, u32[]{:S(2)}, u32[]{:S(2)}) collective-permute-start(f32[16,16,5,128]{3,1,2,0:T(8,128)S(1)} %copy.21), channel_id=1, source_target_pairs={{1,0},{2,1},{3,2},{4,3},{5,4},{6,5},{7,6},{8,7},{9,8},{10,9},{11,1... | collective-permute-start | bytes 1966088 | tf_op jit(solution)/shard_map/ppermute | solution.py:21
  9.8 0.2 copy.20
  10.0 0.1 collective-permute-start
  10.1 0.0 copy-done.6
  10.1 7.8 %collective-permute-done.1 = f32[16,16,5,128]{3,1,2,0:T(8,128)S(1)} collective-permute-done((f32[16,16,5,128]{3,1,2,0:T(8,128)S(1)}, f32[16,16,5,128]{3,1,2,0:T(8,128)S(1)}, u32[]{:S(2)}, u32[]{:S(2)}) %collective-permute-start.1) | collective-permute-done | bytes 655392 | tf_op jit(solution)/shard_map/ppermute | solution.py:21
  17.9 0.2 copy.23
  18.1 4.8 %collective-permute-done = f32[16,16,5,128]{3,1,2,0:T(8,128)S(1)} collective-permute-done((f32[16,16,5,128]{3,1,2,0:T(8,128)S(1)}, f32[16,16,5,128]{3,1,2,0:T(8,128)S(1)}, u32[]{:S(2)}, u32[]{:S(2)}) %collective-permute-start) | collective-permute-done | bytes 655392 | tf_op jit(solution)/shard_map/ppermute | solution.py:18
  22.9 0.2 copy.22
  23.1 0.8 pad_maximum_fusion
  24.0 0.0 copy-start.3
  24.0 0.7 copy-done.3
  24.7 0.0 copy-start
  24.7 0.0 copy-start.1
  24.7 0.0 copy-start.5
  24.7 5.8 %select_add_fusion = f32[16,15,25,128]{3,0,2,1:T(8,128)S(1)} fusion(f32[16,16,29,128]{3,0,2,1:T(8,128)S(1)} %get-tuple-element.47, f32[16,16,29,128]{3,0,2,1:T(8,128)S(1)} %get-tuple-element.46, f32[16,25,128]{2,0,1:T(8,128)S(1)} %get-tuple-element.53, f32[16,25,128]{2,0,1:T(8,128)S(1)} %get-tuple-element.52, f32[16,25,128]{2,0,1:T(8,128)S(1)} %get-tuple-element.51, ...), kind=kLoop, calls=%fused_computation.32 | loop fusion | flops 43776000 | bytes 25196544 | tf_op jit(solution)/shard_map/jvp()/add | solution.py:50
  30.5 0.0 copy-done
  30.5 0.0 copy-done.1
  30.5 0.0 copy-done.5
  30.5 4.3 %multiply_reduce_fusion = (f32[16,15]{0,1:T(8,128)S(1)}, f32[16,15]{0,1:T(8,128)S(1)}, f32[16,15]{0,1:T(8,128)S(1)}, f32[16,15,24,128]{3,0,2,1:T(8,128)}) fusion(f32[16,15,24,128]{3,2,1,0:T(8,128)S(1)} %copy-done.1, f32[24,128]{1,0:T(8,128)S(1)} %copy-done.5, f32[16,15,24,128]{3,2,1,0:T(8,128)S(1)} %copy-done, f32[16,15,25,128]{3,0,2,1:T(8,128)S(1)} %select_add_fusion), kind=kLoop, calls=%fused_computation.40 | loop fusion | flops 8109360 | bytes 14760768 | tf_op jit(solution)/shard_map/reduce_sum | solution.py:74
  34.8 58.1 %all-reduce.18 = (f32[16,15]{0,1:T(8,128)S(1)}, f32[16,15]{0,1:T(8,128)S(1)}, f32[16,15]{0,1:T(8,128)S(1)}) all-reduce(f32[16,15]{0,1:T(8,128)S(1)} %get-tuple-element.8, f32[16,15]{0,1:T(8,128)S(1)} %get-tuple-element.7, f32[16,15]{0,1:T(8,128)S(1)} %get-tuple-element.6), channel_id=1, replica_groups=mesh['group'=2,'tile'=16] {'tile'}, use_global_device_ids=true, to_apply=%region_1.2 | all-reduce | flops 720 | bytes 5760 | tf_op jit(solution)/shard_map/psum | solution.py:70
  92.9 0.0 copy-start.4
  92.9 6.6 %fusion.15 = (f32[16,15,24,128]{3,0,2,1:T(8,128)S(1)}, f32[16,15,24,128]{3,0,2,1:T(8,128)S(1)}, f32[16,15,24,128]{3,0,2,1:T(8,128)}, f32[16,15,24,128]{3,0,2,1:T(8,128)}) fusion(f32[24,128]{1,0:T(8,128)S(1)} %copy-done.5, f32[16,15,24,128]{3,0,2,1:T(8,128)} %get-tuple-element.23, f32[16,15]{0,1:T(8,128)S(1)} %get-tuple-element.55, ...), kind=kLoop, calls=%fused_computation.69 | loop fusion | flops 8110080 | bytes 17708928 | tf_op jit(solution)/shard_map/transpose(jvp())/neg | solution.py:53
  99.5 0.0 copy-done.4
  99.5 1.1 negate_multiply_fusion.9
  100.6 17.7 %add_add_fusion.4 = (f32[16,15,25,128]{3,0,2,1:T(8,128)S(1)}, f32[16,15,25,128]{3,0,2,1:T(8,128)}, f32[16,15,25,128]{3,0,2,1:T(8,128)}, f32[16,15,25,128]{3,0,2,...) fusion(f32[16,15,25,128]{3,0,2,1:T(8,128)S(1)} %get-tuple-eleme, ...), kind=kLoop, calls=%fused_computation.24 | loop fusion | flops 52992000 | bytes 46700544 | tf_op jit(solution)/shard_map/transpose(jvp())/add_any | solution.py:43
  118.4 0.0 copy-start.2
  118.4 14.7 %pad_add_fusion = f32[16,15,34,128]{3,0,2,1:T(8,128)S(1)} fusion(f32[16,15,25,128]{3,0,2,1:T(8,128)} %get-tuple-element.36, f32[16,15,25,128]{3,0,2,1:T(8,128)} %get-tuple-element.37, f32[16,15,25,128]{3,0,2,1:T(8,128)} %get-tuple-element.38, f32[16,15,25,128]{3,0,2,1:T(8,128)} %get-tuple-element.35, f32[16,15,25,128]{3,0,2,1:T(8,128)} %get-tuple-element.34, ...), kind=kLoop, calls=%fused_computation | loop fusion | flops 15667200 | bytes 53207040 | tf_op jit(solution)/shard_map/transpose(jvp())/add_any | solution.py:32
  133.1 0.1 fusion.17
  133.2 0.1 collective-permute-start.3
  133.2 0.5 collective-permute-start.2
  133.7 0.1 pad.73.clone
  133.8 0.0 copy-done.2
  133.8 2.5 %copy.30 = f32[16,15,24,128]{3,2,1,0:T(8,128)} copy(f32[16,15,24,128]{3,0,2,1:T(8,128)S(1)} %copy-done.2) | data formatting | bytes 5898240
  136.3 4.6 %collective-permute-done.3 = f32[16,15,5,128]{3,0,2,1:T(8,128)S(1)} collective-permute-done((f32[16,15,5,128]{3,0,2,1:T(8,128)S(1)}, f32[16,15,5,128]{3,0,2,1:T(8,128)S(1)}, u32[]{:S(2)}, u32[]{:S(2)}) %collective-permute-start.3) | collective-permute-done | bytes 614432 | tf_op jit(solution)/shard_map/ppermute | solution.py:21
  140.9 4.7 %collective-permute-done.2 = f32[16,15,5,128]{3,0,2,1:T(8,128)S(1)} collective-permute-done((f32[16,15,5,128]{3,0,2,1:T(8,128)S(1)}, f32[16,15,5,128]{3,0,2,1:T(8,128)S(1)}, u32[]{:S(2)}, u32[]{:S(2)}) %collective-permute-start.2) | collective-permute-done | bytes 614432 | tf_op jit(solution)/shard_map/ppermute | solution.py:18
  145.6 0.5 fusion.7
  146.1 2.5 %copy.31 = f32[16,15,24,128]{3,2,1,0:T(8,128)} copy(f32[16,15,24,128]{3,0,2,1:T(8,128)S(1)} %fusion.7) | data formatting | bytes 5898240
  (5 shorter events, 0.1 us)
Async XLA Ops:
  3.9 6.1 %copy-start.6 = (s32[16,128]{1,0:T(8,128)S(1)}, s32[16,128]{1,0:T(8,128)}, u32[]{:S(2)}) copy-start(s32[16,128]{1,0:T(8,128)} %param.7) | copy-start | bytes 24580
  4.3 13.6 %collective-permute-start.1 = (f32[16,16,5,128]{3,1,2,0:T(8,128)S(1)}, f32[16,16,5,128]{3,1,2,0:T(8,128)S(1)}, u32[]{:S(2)}, u32[]{:S(2)}) collective-permute-start(f32[16,16,5,128]{3,1,2,0:T(8,128)S(1)} %copy.21), channel_id=1, source_target_pairs={{1,0},{2,1},{3,2},{4,3},{5,4},{6,5},{7,6},{8,7},{9,8},{10,9},{11,1... | collective-permute-start | bytes 1966088 | tf_op jit(solution)/shard_map/ppermute | solution.py:21
  10.0 12.9 %collective-permute-start = (f32[16,16,5,128]{3,1,2,0:T(8,128)S(1)}, f32[16,16,5,128]{3,1,2,0:T(8,128)S(1)}, u32[]{:S(2)}, u32[]{:S(2)}) collective-permute-start(f32[16,16,5,128]{3,1,2,0:T(8,128)S(1)} %copy.20), channel_id=1, source_target_pairs={{0,1},{1,2},{2,3},{3,4},{4,5},{5,6},{6,7},{7,8},{8,9},{9,10},{10,1... | collective-permute-start | bytes 1966088 | tf_op jit(solution)/shard_map/ppermute | solution.py:18
  24.0 0.7 copy-start.3
  24.7 5.8 %copy-start = (f32[16,15,24,128]{3,2,1,0:T(8,128)S(1)}, f32[16,15,24,128]{3,2,1,0:T(8,128)}, u32[]{:S(2)}) copy-start(f32[16,15,24,128]{3,2,1,0:T(8,128)} %param.5) | copy-start | bytes 8847364
  24.7 5.8 %copy-start.1 = (f32[16,15,24,128]{3,2,1,0:T(8,128)S(1)}, f32[16,15,24,128]{3,2,1,0:T(8,128)}, u32[]{:S(2)}) copy-start(f32[16,15,24,128]{3,2,1,0:T(8,128)} %param.9) | copy-start | bytes 8847364
  24.7 5.8 %copy-start.5 = (f32[24,128]{1,0:T(8,128)S(1)}, f32[24,128]{1,0:T(8,128)}, u32[]{:S(2)}) copy-start(f32[24,128]{1,0:T(8,128)} %param.8) | copy-start | bytes 36868
  92.9 6.7 %copy-start.4 = (f32[16,25,128]{2,0,1:T(8,128)S(1)}, f32[16,25,128]{2,0,1:T(8,128)}, u32[]{:S(2)}) copy-start(f32[16,25,128]{2,0,1:T(8,128)} %copy-done.3) | copy-start | bytes 614404
  118.4 15.5 %copy-start.2 = (f32[16,15,24,128]{3,0,2,1:T(8,128)S(1)}, f32[16,15,24,128]{3,0,2,1:T(8,128)}, u32[]{:S(2)}) copy-start(f32[16,15,24,128]{3,0,2,1:T(8,128)} %get-tuple-element.50) | copy-start | bytes 8847364
  133.2 7.7 %collective-permute-start.3 = (f32[16,15,5,128]{3,0,2,1:T(8,128)S(1)}, f32[16,15,5,128]{3,0,2,1:T(8,128)S(1)}, u32[]{:S(2)}, u32[]{:S(2)}) collective-permute-start(f32[16,15,5,128]{3,0,2,1:T(8,128)S(1)} %get-tuple-element.25), channel_id=1, source_target_pairs={{1,0},{2,1},{3,2},{4,3},{5,4},{6,5},{7,6},{8,7},{9,8},{10,9},{11,1... | collective-permute-start | bytes 1843208 | tf_op jit(solution)/shard_map/ppermute | solution.py:21
  133.2 12.3 %collective-permute-start.2 = (f32[16,15,5,128]{3,0,2,1:T(8,128)S(1)}, f32[16,15,5,128]{3,0,2,1:T(8,128)S(1)}, u32[]{:S(2)}, u32[]{:S(2)}) collective-permute-start(f32[16,15,5,128]{3,0,2,1:T(8,128)S(1)} %get-tuple-element.24), channel_id=1, source_target_pairs={{0,1},{1,2},{2,3},{3,4},{4,5},{5,6},{6,7},{7,8},{8,9},{9,10},{10,1... | collective-permute-start | bytes 1843208 | tf_op jit(solution)/shard_map/ppermute | solution.py:18
where the time goes:
time: 149 us
  blocking collectives  58.1 us (39%)
  other arithmetic  51.8 us (35%)
  waiting for transfers between devices  21.8 us (15%)
  local copies, waits for them, and re-layouts  10.1 us (7%)
  starting transfers between devices  6.11 us (4%)
    psum x1, blocking collectives, shards(): lax.psum((jnp.sum(cell_area * tracer, axis=(2, 3)), jnp.sum(cell_area * p...  58.1 us
    add_any x1, other arithmetic, advect(): center + plus_one  17.7 us
    add_any x1, other arithmetic, take_faces(): return window[:, :, position:position + face_count, :]  14.7 us
    ppermute x2, waiting for transfers between devices, extended_2(): lax.ppermute(lax.slice_in_dim(block, 0, width, axis=dim), axis, backward)  12.4 us
    ppermute x2, waiting for transfers between devices, extended_2(): lax.ppermute(lax.slice_in_dim(block, block.shape[dim] - width, None, axis...  9.42 us
    unnamed x18, local copies, waits for them, and re-layouts  9.04 us
    neg x1, other arithmetic, advect(): return interior - (fluxes[:, :, 1:] - fluxes[:, :, :-1]) / area_cells  6.65 us
    add x1, other arithmetic, advect(): fluxes + jnp.where(chosen == shift_count, carried + partial_flux, 0.0)  5.77 us
  transfers between devices with their start and end apart: 4, of which 4 were waited for; matrix products, arithmetic and copies ran while one was open for 2% of the time, Pallas kernels for 0%

commit v1 on v0

v1 whole, which is shorter than its diff:
```python
import jax
import jax.numpy as jnp
from jax import lax
from jax.experimental import pallas as pl
from jax.experimental.pallas import tpu as pltpu
from jax.sharding import PartitionSpec as P

MAXOFF = 2
FLOOR2 = 0.1 * 0.1
LEFT, RIGHT = 3, 2
OFF = MAXOFF
HALO = LEFT + MAXOFF
T = 8
VMEM_LIMIT = 28 * 2**20
HIGHEST = lax.Precision.HIGHEST


def tap_weights(face, west, inverse, shift_is):
    def taps(f):
        f2 = f * f
        f3 = f2 * f
        alpha = 3.0 * f2 - 2.0 * f3
        beta = f3 - f2
        gamma = f - 2.0 * f2 + f3
        return (
            beta * (-1.0 / 12.0),
            (7.0 / 12.0) * beta - (1.0 / 12.0) * gamma,
            alpha + (7.0 / 12.0) * (beta + gamma),
            (7.0 / 12.0) * gamma - (1.0 / 12.0) * beta,
            gamma * (-1.0 / 12.0),
        )

    east_taps, west_taps = taps(face), taps(west)
    weights = [west_taps[0] * inverse]
    for k in range(4):
        weights.append((west_taps[k + 1] - east_taps[k]) * inverse)
    weights.append(-east_taps[4] * inverse)
    is0, is1, is2 = shift_is
    rest = 1.0 - inverse
    weights[3] = weights[3] + jnp.where(is0, 1.0, inverse)
    weights[4] = weights[4] + jnp.where(is1, rest, 0.0)
    weights[5] = weights[5] + jnp.where(is2, rest, 0.0)
    return weights


def masks(shift_ref, level):
    n = jnp.broadcast_to(shift_ref[pl.ds(level, 1), :], (T, shift_ref.shape[1]))
    return n == 0, n == 1, n == 2


def pick(load, start, shift_is):
    return jnp.where(
        shift_is[0], load(start), jnp.where(shift_is[1], load(start + 1), load(start + 2))
    )


def pick_back(load, start, shift_is):
    return jnp.where(
        shift_is[0], load(start), jnp.where(shift_is[1], load(start - 1), load(start - 2))
    )


def fir(weights, load, start):
    total = weights[0] * load(start)
    for k in range(1, LEFT + RIGHT + 1):
        total = total + weights[k] * load(start + k)
    return total


def floor_parts(advected):
    square = advected * advected + FLOOR2
    root = lax.rsqrt(square)
    return square * root, advected * root


def pack_right_kernel(t_hbm, s_hbm, f_ref, area_ref, out_ref, t_buf, s_buf, sems):
    count, columns, _ = t_hbm.shape
    levels = f_ref.shape[0]
    copies = [
        pltpu.make_async_copy(t_hbm.at[:, pl.ds(columns - T, T), :], t_buf, sems.at[0]),
        pltpu.make_async_copy(s_hbm.at[:, pl.ds(columns - T, T), :], s_buf, sems.at[1]),
    ]
    for copy in copies:
        copy.start()
    width = HALO + MAXOFF
    out_ref[0:T, :] = jnp.zeros((T, out_ref.shape[1]), jnp.float32)
    for copy in copies:
        copy.wait()

    def body(lb, _):
        row = T + lb * width
        out_ref[pl.ds(row + HALO, MAXOFF), :] = s_buf[lb, T - MAXOFF : T, :]
        out_ref[pl.ds(row, HALO), :] = t_buf[lb, T - HALO : T, :]
        return 0

    lax.fori_loop(0, count, body, 0, unroll=8)
    row = T + count * width
    for level in range(levels):
        out_ref[row + LEFT * level : row + LEFT * (level + 1), :] = f_ref[level, columns - LEFT : columns, :]
    row = row + LEFT * levels
    out_ref[row : row + MAXOFF, :] = area_ref[columns - MAXOFF : columns, :]
    end = out_ref.shape[0]
    out_ref[row + MAXOFF : end, :] = jnp.zeros((end - row - MAXOFF, out_ref.shape[1]), jnp.float32)


def interior_kernel(
    t_hbm, s_hbm, f_ref, area_ref, n_ref,
    tv_ref, sv_ref, adv_ref, w_ref, ap_ref, red_ref, out_ref,
    part, sems,
):
    count, columns, rows = t_hbm.shape
    levels = f_ref.shape[0]
    bins = count // levels
    chunks = 4
    per = levels // chunks
    copies = []
    for c in range(chunks):
        span = pl.ds(c * per * bins, per * bins)
        copies.append(
            (
                pltpu.make_async_copy(t_hbm.at[span], tv_ref.at[span, pl.ds(T, columns), :], sems.at[0, c]),
                pltpu.make_async_copy(s_hbm.at[span], sv_ref.at[span, pl.ds(T, columns), :], sems.at[1, c]),
            )
        )
        copies[c][0].start()
        copies[c][1].start()

    tiles = range(1, columns // T)
    width = 2 * HALO

    def level_body(level, _):
        shift_is = masks(n_ref, level)
        weights, areas = [], []
        for v in tiles:
            cell = T * v - OFF
            face = pick(lambda r: f_ref[level, pl.ds(r, T), :], cell, shift_is)
            west = pick(lambda r: f_ref[level, pl.ds(r, T), :], cell - 1, shift_is)
            area = pick(lambda r: area_ref[pl.ds(r, T), :], cell, shift_is)
            w = tap_weights(face, west, 1.0 / area, shift_is)
            for k, value in enumerate(w):
                w_ref[level, k, pl.ds(T * v, T), :] = value
            ap_ref[level, pl.ds(T * v, T), :] = area
            weights.append(w)
            areas.append(area)

        def bin_body(b, _):
            lb = level * bins + b
            mass = area_ref[0:T, :] * tv_ref[lb, T : 2 * T, :]
            for v in range(1, columns // T):
                mass = mass + area_ref[T * v : T * v + T, :] * tv_ref[lb, T * v + T : T * v + 2 * T, :]
            after = dot = None
            for v, w, area in zip(tiles, weights, areas):
                cell = T * v - OFF
                advected = fir(w, lambda r: tv_ref[lb, pl.ds(T + r, T), :], cell - LEFT)
                adv_ref[lb, pl.ds(T * v, T), :] = advected
                positive, _ = floor_parts(advected)
                seed = pick(lambda r: sv_ref[lb, pl.ds(T + r, T), :], cell, shift_is)
                after = area * positive if after is None else after + area * positive
                dot = seed * positive if dot is None else dot + seed * positive
            for k, value in enumerate((mass, after, dot)):
                part[k, pl.ds(lb * T, T), :] = value
            row = T + lb * width
            out_ref[pl.ds(row, HALO), :] = tv_ref[lb, T : T + HALO, :]
            out_ref[pl.ds(row + HALO, HALO), :] = sv_ref[lb, T : T + HALO, :]
            return 0

        lax.fori_loop(0, bins, bin_body, 0, unroll=3)
        return 0

    for c in range(chunks):
        copies[c][0].wait()
        copies[c][1].wait()
        lax.fori_loop(c * per, (c + 1) * per, level_body, 0)

    out_ref[0:T, :] = jnp.zeros((T, rows), jnp.float32)
    row = T + count * width
    for level in range(levels):
        out_ref[row + HALO * level : row + HALO * (level + 1), :] = f_ref[level, 0:HALO, :]
    row = row + HALO * levels
    out_ref[row : row + HALO, :] = area_ref[0:HALO, :]
    end = out_ref.shape[0]
    out_ref[row + HALO : end, :] = jnp.zeros((end - row - HALO, rows), jnp.float32)

    reduce_rows(part, red_ref, 3, count)


def reduce_rows(part, red_ref, kinds, count):
    def body(g, _):
        for k in range(kinds):
            total = part[k, pl.ds(g * T * T, T, stride=T), :]
            for s in range(1, T):
                total = total + part[k, pl.ds(g * T * T + s, T, stride=T), :]
            red_ref[k, pl.ds(g * T, T), :] = total
        return 0

    lax.fori_loop(0, count // T, body, 0, unroll=2)


def left_kernel(
    m_ref, tv_in, sv_in, adv_in, w_in, ap_in, red_ref, f_ref, area_ref, n_ref,
    tv_ref, sv_ref, adv_ref, w_ref, ap_ref, sum_ref,
    part, red_new, f_buf, area_buf,
):
    count = tv_ref.shape[0]
    levels = f_ref.shape[0]
    bins = count // levels
    rows = f_ref.shape[2]
    width = HALO + MAXOFF
    f_row = T + count * width
    area_row = f_row + LEFT * levels
    area_buf[0:T, :] = m_ref[area_row - (T - MAXOFF) : area_row + MAXOFF, :]
    area_buf[T : 2 * T, :] = area_ref[0:T, :]
    cell = -OFF

    def level_body(level, _):
        shift_is = masks(n_ref, level)
        f_buf[level, 0:T, :] = m_ref[pl.ds(f_row + LEFT * level - (T - LEFT), T), :]
        f_buf[level, T : 2 * T, :] = f_ref[level, 0:T, :]
        face = pick(lambda r: f_buf[level, pl.ds(T + r, T), :], cell, shift_is)
        west = pick(lambda r: f_buf[level, pl.ds(T + r, T), :], cell - 1, shift_is)
        area = pick(lambda r: area_buf[pl.ds(T + r, T), :], cell, shift_is)
        w = tap_weights(face, west, 1.0 / area, shift_is)
        for k, value in enumerate(w):
            w_ref[level, k, 0:T, :] = value
        ap_ref[level, 0:T, :] = area

        def fill_body(b, _):
            lb = level * bins + b
            row = T + lb * width
            tv_ref[lb, 0:T, :] = m_ref[pl.ds(row - (T - HALO), T), :]
            sv_ref[lb, 0:T, :] = m_ref[pl.ds(row + HALO - (T - MAXOFF), T), :]
            return 0

        lax.fori_loop(0, bins, fill_body, 0, unroll=True)

        def bin_body(b, _):
            lb = level * bins + b
            advected = fir(w, lambda r: tv_ref[lb, pl.ds(T + r, T), :], cell - LEFT)
            adv_ref[lb, 0:T, :] = advected
            positive, _ = floor_parts(advected)
            seed = pick(lambda r: sv_ref[lb, pl.ds(T + r, T), :], cell, shift_is)
            part[0, pl.ds(lb * T, T), :] = area * positive
            part[1, pl.ds(lb * T, T), :] = seed * positive
            return 0

        lax.fori_loop(0, bins, bin_body, 0, unroll=5)
        return 0

    lax.fori_loop(0, levels, level_body, 0)
    reduce_rows(part, red_new, 2, count)
    ones = jnp.ones((T, rows), jnp.float32)
    for k in range(3):
        values = red_ref[k] if k == 0 else red_ref[k] + red_new[k - 1]
        total = lax.dot_general(
            ones, values, (((1,), (1,)), ((), ())), precision=HIGHEST, preferred_element_type=jnp.float32
        )
        for peer in range(sum_ref.shape[0]):
            sum_ref[peer, k : k + 1, :] = total[0:1, :]


def main_kernel(
    g_ref, sv_ref, adv_ref, w_ref, ap_ref, area_ref, n_ref,
    next_hbm, adj_hbm, scale_ref,
    s_buf, next_buf, adj_buf, sems,
):
    count, rows = scale_ref.shape[1:]
    levels = n_ref.shape[0]
    bins = count // levels
    peers = g_ref.shape[0]
    tiles = next_buf.shape[1] // T
    ones = jnp.ones((peers, rows), jnp.float32)
    sums = [
        lax.dot_general(
            g_ref[:, k, :], ones, (((0,), (0,)), ((), ())), precision=HIGHEST, preferred_element_type=jnp.float32
        )
        for k in range(3)
    ]
    mass_before, mass_after, seed_dot = sums
    direct = seed_dot / mass_after
    rescale = mass_before / mass_after
    scale_ref[0] = rescale
    scale_ref[1] = rescale * direct
    scale_ref[2] = direct

    def copies(level):
        span = pl.ds(level * bins, bins)
        return (
            pltpu.make_async_copy(next_buf.at[span], next_hbm.at[span, pl.ds(0, tiles * T), :], sems.at[0, level]),
            pltpu.make_async_copy(adj_buf.at[span], adj_hbm.at[span, pl.ds(0, tiles * T), :], sems.at[1, level]),
        )

    def level_body(level, _):
        shift_is = masks(n_ref, level)
        areas = [ap_ref[level, T * v : T * v + T, :] for v in range(tiles + 1)]

        def seed_body(b, _):
            lb = level * bins + b
            rescale = scale_ref[0, pl.ds(lb, 1), :]
            feedback = scale_ref[1, pl.ds(lb, 1), :]
            for v in range(tiles + 1):
                _, ratio = floor_parts(adv_ref[lb, T * v : T * v + T, :])
                seed = pick(lambda r: sv_ref[lb, pl.ds(T + r, T), :], T * v - OFF, shift_is)
                s_buf[b, T * v : T * v + T, :] = (rescale * seed - feedback * areas[v]) * ratio
            return 0

        lax.fori_loop(0, bins, seed_body, 0, unroll=3)
        weights = [
            [w_ref[level, k, pl.ds(T * q + OFF + LEFT - k, T), :] for k in range(LEFT + RIGHT + 1)]
            for q in range(tiles)
        ]

        def bin_body(b, _):
            lb = level * bins + b
            rescale = scale_ref[0, pl.ds(lb, 1), :]
            direct = scale_ref[2, pl.ds(lb, 1), :]
            for q in range(tiles):
                total = area_ref[T * q : T * q + T, :] * direct
                for k in range(LEFT + RIGHT + 1):
                    total = total + weights[q][k] * s_buf[b, pl.ds(T * q + OFF + LEFT - k, T), :]
                adj_buf[lb, T * q : T * q + T, :] = total
                advected = pick_back(lambda r: adv_ref[lb, pl.ds(r, T), :], T * q + OFF, shift_is)
                positive, _ = floor_parts(advected)
                next_buf[lb, T * q : T * q + T, :] = positive * rescale
            return 0

        lax.fori_loop(0, bins, bin_body, 0, unroll=3)
        for copy in copies(level):
            copy.start()
        return 0

    lax.fori_loop(0, levels, level_body, 0)

    def wait_body(level, _):
        for copy in copies(level):
            copy.wait()
        return 0

    lax.fori_loop(0, levels, wait_body, 0)


def right_kernel(
    m_ref, tv_ref, sv_ref, adv_ref, w_ref, ap_ref, scale_ref, f_ref, area_ref, n_ref, next_in, adj_in,
    next_hbm, adj_hbm,
    t_buf, seed_buf, adv_buf, w_buf, f_buf, area_buf, s_buf, next_buf, adj_buf, sems,
):
    count = tv_ref.shape[0]
    levels, columns, rows = f_ref.shape
    bins = count // levels
    width = 2 * HALO
    f_row = T + count * width
    area_row = f_row + HALO * levels
    last = columns - T
    area_buf[0:T, :] = area_ref[last:columns, :]
    area_buf[T : 2 * T, :] = m_ref[area_row : area_row + T, :]
    cell = T - OFF

    def copies(level):
        span = pl.ds(level * bins, bins)
        return (
            pltpu.make_async_copy(next_buf.at[span], next_hbm.at[span, pl.ds(last, T), :], sems.at[0, level]),
            pltpu.make_async_copy(adj_buf.at[span], adj_hbm.at[span, pl.ds(last, T), :], sems.at[1, level]),
        )

    def level_body(level, _):
        shift_is = masks(n_ref, level)
        f_buf[level, 0:T, :] = f_ref[level, last:columns, :]
        f_buf[level, T : 2 * T, :] = m_ref[pl.ds(f_row + HALO * level, T), :]
        face = pick(lambda r: f_buf[level, pl.ds(r, T), :], cell, shift_is)
        west = pick(lambda r: f_buf[level, pl.ds(r, T), :], cell - 1, shift_is)
        area = pick(lambda r: area_buf[pl.ds(r, T), :], cell, shift_is)
        w = tap_weights(face, west, 1.0 / area, shift_is)
        for k, value in enumerate(w):
            w_buf[level, k, 0:T, :] = w_ref[level, k, last : last + T, :]
            w_buf[level, k, T : 2 * T, :] = value
        areas = [ap_ref[level, last : last + T, :], area]

        def fill_body(b, _):
            lb = level * bins + b
            row = T + lb * width
            t_buf[b, 0:T, :] = tv_ref[lb, columns : columns + T, :]
            t_buf[b, T : 2 * T, :] = m_ref[pl.ds(row, T), :]
            seed_buf[b, 0:T, :] = sv_ref[lb, columns : columns + T, :]
            seed_buf[b, T : 2 * T, :] = m_ref[pl.ds(row + HALO, T), :]
            adv_buf[b, 0:T, :] = adv_ref[lb, last : last + T, :]
            return 0

        lax.fori_loop(0, bins, fill_body, 0, unroll=True)

        def seed_body(b, _):
            lb = level * bins + b
            rescale = scale_ref[0, pl.ds(lb, 1), :]
            feedback = scale_ref[1, pl.ds(lb, 1), :]
            advected = fir(w, lambda r: t_buf[b, pl.ds(r, T), :], cell - LEFT)
            adv_buf[b, T : 2 * T, :] = advected
            for v, value in enumerate((adv_buf[b, 0:T, :], advected)):
                _, ratio = floor_parts(value)
                if v == 0:
                    seed = pick(lambda r: sv_ref[lb, pl.ds(T + last + r, T), :], -OFF, shift_is)
                else:
                    seed = pick(lambda r: seed_buf[b, pl.ds(r, T), :], cell, shift_is)
                s_buf[b, T * v : T * v + T, :] = (rescale * seed - feedback * areas[v]) * ratio
            return 0

        lax.fori_loop(0, bins, seed_body, 0, unroll=3)
        weights = [w_buf[level, k, pl.ds(OFF + LEFT - k, T), :] for k in range(LEFT + RIGHT + 1)]

        def bin_body(b, _):
            lb = level * bins + b
            rescale = scale_ref[0, pl.ds(lb, 1), :]
            total = area_buf[0:T, :] * scale_ref[2, pl.ds(lb, 1), :]
            for k in range(LEFT + RIGHT + 1):
                total = total + weights[k] * s_buf[b, pl.ds(OFF + LEFT - k, T), :]
            adj_buf[lb] = total
            advected = pick_back(lambda r: adv_buf[b, pl.ds(r, T), :], OFF, shift_is)
            positive, _ = floor_parts(advected)
            next_buf[lb] = positive * rescale
            return 0

        lax.fori_loop(0, bins, bin_body, 0, unroll=3)
        for copy in copies(level):
            copy.start()
        return 0

    lax.fori_loop(0, levels, level_body, 0)

    def wait_body(level, _):
        for copy in copies(level):
            copy.wait()
        return 0

    lax.fori_loop(0, levels, wait_body, 0)


def padded(rows):
    return (rows + 2 * T - 1) // T * T


def shards(tracer, courant_frac, departure_shift, cell_area, adjoint_seed):
    levels, bins, columns, rows = tracer.shape
    count = levels * bins
    f32 = jnp.float32
    tile = lax.axis_size("tile")
    to_right = [(i, (i + 1) % tile) for i in range(tile)]
    to_left = [(target, source) for source, target in to_right]
    t = tracer.reshape(count, columns, rows)
    seed = adjoint_seed.reshape(count, columns, rows)
    hbm = pl.BlockSpec(memory_space=pl.ANY)
    vmem = pl.BlockSpec(memory_space=pltpu.VMEM)
    params = pltpu.CompilerParams(vmem_limit_bytes=VMEM_LIMIT)
    dma = pltpu.SemaphoreType.DMA

    def held(x):
        return pltpu.with_memory_space_constraint(x, pltpu.VMEM)

    def cost(flops, nbytes):
        return pl.CostEstimate(flops=flops, bytes_accessed=nbytes, transcendentals=0)

    right_rows = padded(T + count * (HALO + MAXOFF) + LEFT * levels + MAXOFF)
    left_rows = padded(T + 2 * count * HALO + HALO * levels + HALO)
    size = 4 * count * columns * rows

    message_right = pl.pallas_call(
        pack_right_kernel,
        out_shape=jax.ShapeDtypeStruct((right_rows, rows), f32),
        in_specs=[hbm, hbm, vmem, vmem],
        out_specs=vmem,
        scratch_shapes=[pltpu.VMEM((count, T, rows), f32), pltpu.VMEM((count, T, rows), f32), dma((2,))],
        compiler_params=params,
        cost_estimate=cost(0, size),
        name="pack_right",
    )(t, seed, courant_frac, cell_area)
    from_left = lax.ppermute(message_right, "tile", to_right)

    tv, sv, adv, w, ap, red, message_left = pl.pallas_call(
        interior_kernel,
        out_shape=(
            pltpu.VMEM((count, columns + 2 * T, rows), f32),
            pltpu.VMEM((count, columns + 2 * T, rows), f32),
            pltpu.VMEM((count, columns, rows), f32),
            pltpu.VMEM((levels, LEFT + RIGHT + 1, columns, rows), f32),
            pltpu.VMEM((levels, columns, rows), f32),
            pltpu.VMEM((3, count, rows), f32),
            jax.ShapeDtypeStruct((left_rows, rows), f32),
        ),
        in_specs=[hbm, hbm, vmem, vmem, vmem],
        out_specs=(vmem,) * 7,
        scratch_shapes=[pltpu.VMEM((3, count * T, rows), f32), dma((2, 4))],
        compiler_params=params,
        cost_estimate=cost(30 * size, 4 * size),
        name="interior",
    )(t, seed, courant_frac, cell_area, departure_shift)

    from_left, message_left = lax.optimization_barrier((from_left, message_left))
    from_right = lax.ppermute(message_left, "tile", to_left)

    tv, sv, adv, w, ap, sums = pl.pallas_call(
        left_kernel,
        out_shape=(
            pltpu.VMEM(tv.shape, f32),
            pltpu.VMEM(sv.shape, f32),
            pltpu.VMEM(adv.shape, f32),
            pltpu.VMEM(w.shape, f32),
            pltpu.VMEM(ap.shape, f32),
            jax.ShapeDtypeStruct((tile, 3, count), f32),
        ),
        in_specs=[vmem] * 10,
        out_specs=(vmem,) * 6,
        input_output_aliases={1: 0, 2: 1, 3: 2, 4: 3, 5: 4},
        scratch_shapes=[
            pltpu.VMEM((2, count * T, rows), f32),
            pltpu.VMEM((2, count, rows), f32),
            pltpu.VMEM((levels, 2 * T, rows), f32),
            pltpu.VMEM((2 * T, rows), f32),
        ],
        compiler_params=params,
        cost_estimate=cost(10 * size, size),
        name="left_edge",
    )(from_left, held(tv), held(sv), held(adv), held(w), held(ap), held(red), courant_frac, cell_area, departure_shift)

    sums = lax.all_to_all(sums, "tile", 0, 0)

    main = columns - T
    tracer_next, tracer_adjoint, scale = pl.pallas_call(
        main_kernel,
        out_shape=(
            jax.ShapeDtypeStruct((count, columns, rows), f32),
            jax.ShapeDtypeStruct((count, columns, rows), f32),
            pltpu.VMEM((3, count, rows), f32),
        ),
        in_specs=[vmem] * 7,
        out_specs=(hbm, hbm, vmem),
        scratch_shapes=[
            pltpu.VMEM((bins, columns, rows), f32),
            pltpu.VMEM((count, main, rows), f32),
            pltpu.VMEM((count, main, rows), f32),
            dma((2, levels)),
        ],
        compiler_params=params,
        cost_estimate=cost(30 * size, 4 * size),
        name="main_part",
    )(sums, held(sv), held(adv), held(w), held(ap), cell_area, departure_shift)

    tracer_next, tracer_adjoint = pl.pallas_call(
        right_kernel,
        out_shape=(
            jax.ShapeDtypeStruct((count, columns, rows), f32),
            jax.ShapeDtypeStruct((count, columns, rows), f32),
        ),
        in_specs=[vmem] * 10 + [hbm, hbm],
        out_specs=(hbm, hbm),
        input_output_aliases={10: 0, 11: 1},
        scratch_shapes=[
            pltpu.VMEM((bins, 2 * T, rows), f32),
            pltpu.VMEM((bins, 2 * T, rows), f32),
            pltpu.VMEM((bins, 2 * T, rows), f32),
            pltpu.VMEM((levels, LEFT + RIGHT + 1, 2 * T, rows), f32),
            pltpu.VMEM((levels, 2 * T, rows), f32),
            pltpu.VMEM((2 * T, rows), f32),
            pltpu.VMEM((bins, 2 * T, rows), f32),
            pltpu.VMEM((count, T, rows), f32),
            pltpu.VMEM((count, T, rows), f32),
            dma((2, levels)),
        ],
        compiler_params=params,
        cost_estimate=cost(10 * size, size),
        name="right_edge",
    )(
        from_right, held(tv), held(sv), held(adv), held(w), held(ap), held(scale),
        courant_frac, cell_area, departure_shift, tracer_next, tracer_adjoint,
    )
    return tracer_next.reshape(tracer.shape), tracer_adjoint.reshape(tracer.shape)


def solution(mesh):
    return jax.shard_map(
        shards,
        mesh=mesh,
        in_specs=(
            P("group", None, "tile", None),
            P("group", "tile", None),
            P("group", None),
            P("tile", None),
            P("group", None, "tile", None),
        ),
        out_specs=(P("group", None, "tile", None), P("group", None, "tile", None)),
        check_vma=False,
    )
```

time: 149 us -> 52.4 us (0.35)
  other arithmetic: 51.8 us -> 0 us
  blocking collectives: 58.1 us -> 15.5 us
  Pallas kernels: 0 us -> 18.1 us
  waiting for transfers between devices: 21.8 us -> 12.1 us
  starting transfers between devices: 6.11 us -> 0.51 us
  local copies, waits for them, and re-layouts: 10.1 us -> 5.3 us
    psum x1 -> x0, blocking collectives: 58.1 us -> none  [shards(): lax.psum((jnp.sum(cell_area * tracer, axis=(2, 3)), jnp.sum(cell_area * p...]
    add_any x2 -> x0, other arithmetic: 32.4 us -> none  [the longest x1 17.7 us: advect(): center + plus_one]
    pallas_call x0 -> x5, Pallas kernels: none -> 18.1 us  [the longest x1 5.76 us: shards(): pl.pallas_call(main_kernel, out_shape=(jax.ShapeDtypeStruct((count, colum...]
    all_to_all x0 -> x1, blocking collectives: none -> 15.5 us  [shards(): sums = lax.all_to_all(sums, 'tile', 0, 0)]
    ppermute x4 -> x2, waiting for transfers between devices: 21.8 us -> 12.1 us  [the longest x1 12.1 us: shards(): from_left = lax.ppermute(message_right, 'tile', to_right)]
    neg x1 -> x0, other arithmetic: 6.65 us -> none  [advect(): return interior - (fluxes[:, :, 1:] - fluxes[:, :, :-1]) / area_cells]
    add x2 -> x0, other arithmetic: 6.29 us -> none  [the longest x1 5.77 us: advect(): fluxes + jnp.where(chosen == shift_count, carried + partial_flux, 0.0)]
    ppermute x4 -> x2, starting transfers between devices: 6.11 us -> 0.51 us  [the longest x1 0.5 us: shards(): from_left = lax.ppermute(message_right, 'tile', to_right)]
  transfers between devices with their start and end apart: 4 -> 2, of which waited for: 4 -> 1; matrix products, arithmetic and copies ran while one was open for 2% -> 0% of each run, Pallas kernels for 0% -> 23%
where the time goes in v1:
time: 52.4 us; the launch traced here: 52.1 us
  Pallas kernels  18.1 us (35%)
  blocking collectives  15.5 us (30%)
  waiting for transfers between devices  12.1 us (23%)
  local copies, waits for them, and re-layouts  5.3 us (10%)
  between operations  0.69 us (1%)
    all_to_all x1, blocking collectives, shards(): sums = lax.all_to_all(sums, 'tile', 0, 0)  15.5 us
    ppermute x1, waiting for transfers between devices, shards(): from_left = lax.ppermute(message_right, 'tile', to_right)  12.1 us
    pallas_call x1, Pallas kernels, shards(): pl.pallas_call(main_kernel, out_shape=(jax.ShapeDtypeStruct((count, colum...  5.76 us
    pallas_call x1, Pallas kernels, shards(): pl.pallas_call(right_kernel, out_shape=(jax.ShapeDtypeStruct((count, colu...  5.47 us
    unnamed x10, local copies, waits for them, and re-layouts  5.3 us
    pallas_call x1, Pallas kernels, shards(): pl.pallas_call(interior_kernel, out_shape=(pltpu.VMEM((count, columns + 2...  3.77 us
    pallas_call x1, Pallas kernels, shards(): pl.pallas_call(left_kernel, out_shape=(pltpu.VMEM(tv.shape, f32), pltpu.V...  2.62 us
  transfers between devices with their start and end apart: 2, of which 1 were waited for; matrix products, arithmetic and copies ran while one was open for 0% of the time, Pallas kernels for 23%

profile of v1, /device:TPU:0, one launch (start us, length us, event | category | flops | bytes accessed | tf_op | source)
XLA Modules:
  0.0 52.1 jit_solution(11272461288577786945)
XLA Ops:
  0.6 0.0 copy-start
  0.6 1.8 %copy-done = f32[16,15,24,128]{3,2,1,0:T(8,128)S(1)} copy-done((f32[16,15,24,128]{3,2,1,0:T(8,128)S(1)}, f32[16,15,24,128]{3,2,1,0:T(8,128)}, u32[]{:S(2)}) %copy-start) | copy-done | bytes 2949144
  2.5 0.0 copy-start.1
  2.5 1.8 %copy-done.1 = f32[16,15,24,128]{3,2,1,0:T(8,128)S(1)} copy-done((f32[16,15,24,128]{3,2,1,0:T(8,128)S(1)}, f32[16,15,24,128]{3,2,1,0:T(8,128)}, u32[]{:S(2)}) %copy-start.1) | copy-done | bytes 2949144
  4.3 0.0 copy-start.2
  4.3 0.9 %copy-done.2 = f32[16,24,128]{2,1,0:T(8,128)S(1)} copy-done((f32[16,24,128]{2,1,0:T(8,128)S(1)}, f32[16,24,128]{2,1,0:T(8,128)}, u32[]{:S(2)}) %copy-start.2) | copy-done | bytes 196632
  5.2 0.0 copy-start.3
  5.2 0.7 %copy-done.3 = f32[24,128]{1,0:T(8,128)S(1)} copy-done((f32[24,128]{1,0:T(8,128)S(1)}, f32[24,128]{1,0:T(8,128)}, u32[]{:S(2)}) %copy-start.3) | copy-done | bytes 12312
  5.9 0.0 copy-start.4
  5.9 0.5 pack_right.1
  6.4 0.5 collective-permute-start
  6.9 0.0 copy-done.4
  6.9 3.8 %interior.1 = (f32[240,40,128]{2,1,0:T(8,128)S(1)}, f32[240,40,128]{2,1,0:T(8,128)S(1)}, f32[240,24,128]{2,1,0:T(8,128)S(1)}, f32[16,6,24,128]{3,2,1,0:T(8,128)S...) custom-call(f32[240,24,128]{2,1,0:T(8,128)S(1)} %bitcast.5, ...), custom_call_target="tpu_custom_call" | custom-call | flops 88473600 | bytes 11796480 | tf_op jit(solution)/shard_map/interior/pallas_call | solution.py:474
  10.7 12.1 %collective-permute-done.m_ref = f32[1752,128]{1,0:T(8,128)S(1)} collective-permute-done((f32[1752,128]{1,0:T(8,128)S(1)}, f32[1752,128]{1,0:T(8,128)S(1)}, u32[]{:S(2)}, u32[]{:S(2)}) %collective-permute-start) | collective-permute-done | bytes 897056 | tf_op jit(solution)/shard_map/ppermute | solution.py:472
  22.8 0.0 collective-permute-start.1
  22.8 2.6 %left_edge.1 = (f32[240,40,128]{2,1,0:T(8,128)S(1)}, f32[240,40,128]{2,1,0:T(8,128)S(1)}, f32[240,24,128]{2,1,0:T(8,128)S(1)}, f32[16,6,24,128]{3,2,1,0:T(8,128)...) custom-call(f32[1752,128]{1,0:T(8,128)S(1)} %collective-permute-done, ...), custom_call_target="tpu_custom_call", output_to_operand_aliasing={{0}: (1, {}), {1}: (2, {}), {2}: (3, {}), {3}: (4, {}), {4}... | custom-call | flops 29491200 | bytes 2949120 | tf_op jit(solution)/shard_map/left_edge/pallas_call | solution.py:496
  25.4 15.5 %all_to_all.5.g_ref = f32[16,3,240]{2,1,0:T(4,128)S(1)} all-to-all(f32[16,3,240]{2,1,0:T(4,128)S(1)} %get-tuple-element.36), channel_id=1, replica_groups=mesh['group'=2,'tile'=16] {'tile'}, dimensions={0} | all-to-all | bytes 92160 | tf_op jit(solution)/shard_map/all_to_all | solution.py:520
  40.9 5.8 %main_part.1 = (f32[240,24,128]{2,1,0:T(8,128)}, f32[240,24,128]{2,1,0:T(8,128)}, f32[3,240,128]{2,1,0:T(8,128)S(1)}) custom-call(f32[16,3,240]{2,1,0:T(4,128)S(1)} %all_to_all.5.g_ref, f32[240,40,128]{2,1,0:T(8,128)S(1)} %get-tuple-element.32.sv_ref, f32[240,24,128]{2,1,0:T(8,128)S(1)} %get-tuple-element.33.adv_ref, ...), custom_call_target="tpu_custom_call" | custom-call | flops 88473600 | bytes 11796480 | tf_op jit(solution)/shard_map/main_part/pallas_call | solution.py:523
  46.7 0.0 collective-permute-done.1.m_ref
  46.7 5.5 %right_edge.1 = (f32[240,24,128]{2,1,0:T(8,128)}, f32[240,24,128]{2,1,0:T(8,128)}) custom-call(f32[2504,128]{1,0:T(8,128)S(1)} %collective-permute-done.1.m_ref, f32[240,40,128]{2,1,0:T(8,128)S(1)} %get-tuple-element.31.tv_ref, f32[240,40,128]{2,1,0:T(8,128)S(1)} %get-tuple-element.32.sv_ref, ...), custom_call_target="tpu_custom_call", output_to_operand_aliasing={{0}: (10, {}), {1}: (11, {})} | custom-call | flops 29491200 | bytes 2949120 | tf_op jit(solution)/shard_map/right_edge/pallas_call | solution.py:543
Async XLA Ops:
  0.6 1.8 %copy-start = (f32[16,15,24,128]{3,2,1,0:T(8,128)S(1)}, f32[16,15,24,128]{3,2,1,0:T(8,128)}, u32[]{:S(2)}) copy-start(f32[16,15,24,128]{3,2,1,0:T(8,128)} %param.5) | copy-start | bytes 8847364
  2.5 1.8 %copy-start.1 = (f32[16,15,24,128]{3,2,1,0:T(8,128)S(1)}, f32[16,15,24,128]{3,2,1,0:T(8,128)}, u32[]{:S(2)}) copy-start(f32[16,15,24,128]{3,2,1,0:T(8,128)} %param.9) | copy-start | bytes 8847364
  4.3 0.9 %copy-start.2 = (f32[16,24,128]{2,1,0:T(8,128)S(1)}, f32[16,24,128]{2,1,0:T(8,128)}, u32[]{:S(2)}) copy-start(f32[16,24,128]{2,1,0:T(8,128)} %f_ref.7) | copy-start | bytes 589828
  5.2 0.7 %copy-start.3 = (f32[24,128]{1,0:T(8,128)S(1)}, f32[24,128]{1,0:T(8,128)}, u32[]{:S(2)}) copy-start(f32[24,128]{1,0:T(8,128)} %area_ref.9) | copy-start | bytes 36868
  5.9 1.0 %copy-start.4 = (s32[16,128]{1,0:T(8,128)S(1)}, s32[16,128]{1,0:T(8,128)}, u32[]{:S(2)}) copy-start(s32[16,128]{1,0:T(8,128)} %n_ref.7) | copy-start | bytes 24580
  6.4 16.4 %collective-permute-start = (f32[1752,128]{1,0:T(8,128)S(1)}, f32[1752,128]{1,0:T(8,128)S(1)}, u32[]{:S(2)}, u32[]{:S(2)}) collective-permute-start(f32[1752,128]{1,0:T(8,128)S(1)} %pack_right.1), channel_id=1, source_target_pairs={{0,1},{1,2},{2,3},{3,4},{4,5},{5,6},{6,7},{7,8},{8,9},{9,10},{10,1... | collective-permute-start | bytes 2691080 | tf_op jit(solution)/shard_map/ppermute | solution.py:472
  22.8 23.9 %collective-permute-start.1 = (f32[2504,128]{1,0:T(8,128)S(1)}, f32[2504,128]{1,0:T(8,128)S(1)}, u32[]{:S(2)}, u32[]{:S(2)}) collective-permute-start(f32[2504,128]{1,0:T(8,128)S(1)} %get-tuple-element.23), channel_id=1, source_target_pairs={{1,0},{2,1},{3,2},{4,3},{5,4},{6,5},{7,6},{8,7},{9,8},{10,9},{11,1... | collective-permute-start | bytes 3846152 | tf_op jit(solution)/shard_map/ppermute | solution.py:494

commit v2 on v1

v2 whole, which is shorter than its diff:
```python
import jax
import jax.numpy as jnp
from jax import lax
from jax.experimental import pallas as pl
from jax.experimental.pallas import tpu as pltpu
from jax.sharding import PartitionSpec as P

MAXOFF = 2
FLOOR2 = 0.1 * 0.1
LEFT, RIGHT = 3, 2
OFF = MAXOFF
HALO = LEFT + MAXOFF
T = 8
VMEM_LIMIT = 20 * 2**20
MAIN_FLOPS = 3000
HIGHEST = lax.Precision.HIGHEST


def tap_weights(face, west, inverse, shift_is):
    def taps(f):
        f2 = f * f
        f3 = f2 * f
        alpha = 3.0 * f2 - 2.0 * f3
        beta = f3 - f2
        gamma = f - 2.0 * f2 + f3
        return (
            beta * (-1.0 / 12.0),
            (7.0 / 12.0) * beta - (1.0 / 12.0) * gamma,
            alpha + (7.0 / 12.0) * (beta + gamma),
            (7.0 / 12.0) * gamma - (1.0 / 12.0) * beta,
            gamma * (-1.0 / 12.0),
        )

    east_taps, west_taps = taps(face), taps(west)
    weights = [west_taps[0] * inverse]
    for k in range(4):
        weights.append((west_taps[k + 1] - east_taps[k]) * inverse)
    weights.append(-east_taps[4] * inverse)
    is0, is1, is2 = shift_is
    rest = 1.0 - inverse
    weights[3] = weights[3] + jnp.where(is0, 1.0, inverse)
    weights[4] = weights[4] + jnp.where(is1, rest, 0.0)
    weights[5] = weights[5] + jnp.where(is2, rest, 0.0)
    return weights


def masks(shift_ref, level):
    n = jnp.broadcast_to(shift_ref[pl.ds(level, 1), :], (T, shift_ref.shape[1]))
    return n == 0, n == 1, n == 2


def pick(load, start, shift_is):
    return jnp.where(
        shift_is[0], load(start), jnp.where(shift_is[1], load(start + 1), load(start + 2))
    )


def pick_back(load, start, shift_is):
    return jnp.where(
        shift_is[0], load(start), jnp.where(shift_is[1], load(start - 1), load(start - 2))
    )


def pick_first(load, shift_is):
    first = load(0)
    two_down = jnp.concatenate([first[T - 2 : T], first[0 : T - 2]], axis=0)
    one_down = jnp.concatenate([first[T - 1 : T], first[0 : T - 1]], axis=0)
    return jnp.where(shift_is[0], two_down, jnp.where(shift_is[1], one_down, first))


def in_chunks(levels, count):
    edges = [levels * c // count for c in range(count + 1)]
    return list(zip(edges[:-1], edges[1:]))


def fir(weights, load, start):
    total = weights[0] * load(start)
    for k in range(1, LEFT + RIGHT + 1):
        total = total + weights[k] * load(start + k)
    return total


def floor_parts(advected):
    square = advected * advected + FLOOR2
    root = lax.rsqrt(square)
    return square * root, advected * root


def pack_right_kernel(t_hbm, s_hbm, f_hbm, area_hbm, n_hbm, out_ref, t_buf, s_buf, f_buf, area_buf, n_buf, sems, small):
    count, columns, rows = t_hbm.shape
    levels = f_hbm.shape[0]
    bins = count // levels
    chunks = sems.shape[1]
    per = levels // chunks
    tail = pl.ds(columns - T, T)
    others = [
        pltpu.make_async_copy(n_hbm, n_buf, small.at[0]),
        pltpu.make_async_copy(f_hbm.at[:, tail, :], f_buf, small.at[1]),
        pltpu.make_async_copy(area_hbm.at[tail, :], area_buf, small.at[2]),
    ]
    others[0].start()
    copies = []
    for c in range(chunks):
        span = pl.ds(c * per * bins, per * bins)
        copies.append(
            (
                pltpu.make_async_copy(t_hbm.at[span, tail, :], t_buf.at[span], sems.at[0, c]),
                pltpu.make_async_copy(s_hbm.at[span, tail, :], s_buf.at[span], sems.at[1, c]),
            )
        )
        for copy in copies[c]:
            copy.start()
    for copy in others[1:]:
        copy.start()
    width = HALO + MAXOFF
    end = out_ref.shape[0]
    row = T + count * width
    last = row + LEFT * levels
    out_ref[0:T, :] = jnp.zeros((T, rows), jnp.float32)
    out_ref[last + MAXOFF : end, :] = jnp.zeros((end - last - MAXOFF, rows), jnp.float32)
    others[0].wait()

    def level_body(level, _):
        unshifted = n_buf[pl.ds(level, 1), :] == 0
        for b in range(bins):
            lb = level * bins + b
            row = T + lb * width
            out_ref[pl.ds(row, HALO), :] = t_buf[lb, T - HALO : T, :]
            first, second = s_buf[lb, T - 2 : T - 1, :], s_buf[lb, T - 1 : T, :]
            out_ref[pl.ds(row + HALO, 1), :] = jnp.where(unshifted, first, second)
            out_ref[pl.ds(row + HALO + 1, 1), :] = second
        return 0

    for c in range(chunks):
        for copy in copies[c]:
            copy.wait()
        lax.fori_loop(c * per, (c + 1) * per, level_body, 0)
    for copy in others[1:]:
        copy.wait()
    for level in range(levels):
        out_ref[row + LEFT * level : row + LEFT * (level + 1), :] = f_buf[level, T - LEFT : T, :]
    out_ref[last : last + MAXOFF, :] = area_buf[T - MAXOFF : T, :]


def interior_kernel(
    t_hbm, s_hbm, f_ref, area_ref, n_ref,
    t0_ref, s0_ref, adv_hbm, seed_hbm, w_ref, ap_ref, red_ref,
    t_buf, s_buf, adv_ref, seed_ref, part, sems, out_sems,
):
    count, columns, _ = t_hbm.shape
    levels = f_ref.shape[0]
    bins = count // levels
    chunks = 4
    per = levels // chunks
    copies = []
    for c in range(chunks):
        span = pl.ds(c * per * bins, per * bins)
        copies.append(
            (
                pltpu.make_async_copy(t_hbm.at[span], t_buf.at[span], sems.at[0, c]),
                pltpu.make_async_copy(s_hbm.at[span], s_buf.at[span], sems.at[1, c]),
            )
        )
        copies[c][0].start()
        copies[c][1].start()

    tiles = range(1, columns // T)

    def copies_out(c):
        span = pl.ds(c * per * bins, per * bins)
        inner = pl.ds(T, columns - T)
        return (
            pltpu.make_async_copy(adv_ref.at[span], adv_hbm.at[span, inner, :], out_sems.at[0, c]),
            pltpu.make_async_copy(seed_ref.at[span], seed_hbm.at[span, inner, :], out_sems.at[1, c]),
        )

    def level_body(level, _):
        shift_is = masks(n_ref, level)
        weights, areas = [], []
        for v in tiles:
            cell = T * v - OFF
            face = pick(lambda r: f_ref[level, pl.ds(r, T), :], cell, shift_is)
            west = pick(lambda r: f_ref[level, pl.ds(r, T), :], cell - 1, shift_is)
            area = pick(lambda r: area_ref[pl.ds(r, T), :], cell, shift_is)
            w = tap_weights(face, west, 1.0 / area, shift_is)
            for k, value in enumerate(w):
                w_ref[level, k, pl.ds(T * v, T), :] = value
            ap_ref[level, pl.ds(T * v, T), :] = area
            weights.append(w)
            areas.append(area)

        def bin_body(b, _):
            lb = level * bins + b
            mass = None
            for v in range(columns // T):
                value = t_buf[lb, T * v : T * v + T, :]
                if v == 0:
                    t0_ref[lb, T : 2 * T, :] = value
                value = area_ref[T * v : T * v + T, :] * value
                mass = value if mass is None else mass + value
            early = pick_first(lambda r: s_buf[lb, pl.ds(r, T), :], shift_is)
            s0_ref[lb] = early
            after = dot = None
            for v, w, area in zip(tiles, weights, areas):
                cell = T * v - OFF
                advected = fir(w, lambda r: t_buf[lb, pl.ds(r, T), :], cell - LEFT)
                adv_ref[lb, pl.ds(T * v - T, T), :] = advected
                positive, _ = floor_parts(advected)
                seed = pick(lambda r: s_buf[lb, pl.ds(r, T), :], cell, shift_is)
                seed_ref[lb, pl.ds(T * v - T, T), :] = seed
                after = area * positive if after is None else after + area * positive
                dot = seed * positive if dot is None else dot + seed * positive
            for k, value in enumerate((mass, after, dot)):
                part[k, pl.ds(lb * T, T), :] = value
            return 0

        lax.fori_loop(0, bins, bin_body, 0, unroll=True)
        return 0

    for c in range(chunks):
        copies[c][0].wait()
        copies[c][1].wait()
        lax.fori_loop(c * per, (c + 1) * per, level_body, 0)
        for copy in copies_out(c):
            copy.start()
    reduce_rows(part, red_ref, 3, count)

    for c in range(chunks):
        for copy in copies_out(c):
            copy.wait()


def reduce_rows(part, red_ref, kinds, count):
    def body(g, _):
        for k in range(kinds):
            total = part[k, pl.ds(g * T * T, T, stride=T), :]
            for s in range(1, T):
                total = total + part[k, pl.ds(g * T * T + s, T, stride=T), :]
            red_ref[k, pl.ds(g * T, T), :] = total
        return 0

    lax.fori_loop(0, count // T, body, 0, unroll=5)


def left_kernel(
    m_ref, t0_in, s0_in, w_in, ap_in, adv_in, seed_in, red_ref, f_ref, area_ref, n_ref,
    t0_ref, w_ref, ap_ref, adv_hbm, seed_hbm, sum_ref, adv_out,
    adv_ref, seed_ref, part, red_new, f_buf, area_buf, sems,
):
    count = t0_ref.shape[0]
    levels, _, rows = f_ref.shape
    bins = count // levels
    width = HALO + MAXOFF
    f_row = T + count * width
    area_row = f_row + LEFT * levels
    area_buf[0:T, :] = m_ref[area_row - (T - MAXOFF) : area_row + MAXOFF, :]
    area_buf[T : 2 * T, :] = area_ref[0:T, :]
    cell = T - OFF
    sublane = lax.broadcasted_iota(jnp.int32, (T, rows), 0)
    chunks = sems.shape[1]
    per = levels // chunks
    copies = []
    for c in range(chunks):
        span = pl.ds(c * per * bins, per * bins)
        copies.append(
            (
                pltpu.make_async_copy(adv_ref.at[span], adv_hbm.at[span, pl.ds(0, T), :], sems.at[0, c]),
                pltpu.make_async_copy(seed_ref.at[span], seed_hbm.at[span, pl.ds(0, T), :], sems.at[1, c]),
            )
        )

    def level_body(level, _):
        shift_is = masks(n_ref, level)
        remote = sublane + jnp.broadcast_to(n_ref[pl.ds(level, 1), :], (T, rows)) < OFF
        f_buf[level, 0:T, :] = m_ref[pl.ds(f_row + LEFT * level - (T - LEFT), T), :]
        f_buf[level, T : 2 * T, :] = f_ref[level, 0:T, :]
        face = pick(lambda r: f_buf[level, pl.ds(r, T), :], cell, shift_is)
        west = pick(lambda r: f_buf[level, pl.ds(r, T), :], cell - 1, shift_is)
        area = pick(lambda r: area_buf[pl.ds(r, T), :], cell, shift_is)
        w = tap_weights(face, west, 1.0 / area, shift_is)
        for k, value in enumerate(w):
            w_ref[level, k, 0:T, :] = value
        ap_ref[level, 0:T, :] = area

        for b in range(bins):
            lb = level * bins + b
            t0_ref[lb, 0:T, :] = m_ref[pl.ds(T + lb * width - (T - HALO), T), :]
        for b in range(bins):
            lb = level * bins + b
            advected = fir(w, lambda r: t0_ref[lb, pl.ds(r, T), :], cell - LEFT)
            adv_ref[lb] = advected
            positive, _ = floor_parts(advected)
            seed = jnp.where(remote, m_ref[pl.ds(T + lb * width + HALO, T), :], s0_in[lb])
            seed_ref[lb] = seed
            part[0, pl.ds(lb * T, T), :] = area * positive
            part[1, pl.ds(lb * T, T), :] = seed * positive
            adv_out[pl.ds(lb * HALO, HALO), :] = advected[0:HALO]
        return 0

    for c in range(chunks):
        lax.fori_loop(c * per, (c + 1) * per, level_body, 0)
        for copy in copies[c]:
            copy.start()
    row = count * HALO
    for level in range(levels):
        adv_out[row + HALO * level : row + HALO * (level + 1), :] = f_ref[level, 0:HALO, :]
    row = row + HALO * levels
    adv_out[row : row + HALO, :] = area_ref[0:HALO, :]
    end = adv_out.shape[0]
    adv_out[row + HALO : end, :] = jnp.zeros((end - row - HALO, rows), jnp.float32)
    reduce_rows(part, red_new, 2, count)
    ones = jnp.ones((T, rows), jnp.float32)
    for k in range(3):
        values = red_ref[k] if k == 0 else red_ref[k] + red_new[k - 1]
        total = lax.dot_general(
            ones, values, (((1,), (1,)), ((), ())), precision=HIGHEST, preferred_element_type=jnp.float32
        )
        for peer in range(sum_ref.shape[0]):
            sum_ref[peer, k : k + 1, :] = total[0:1, :]
    for c in range(chunks):
        for copy in copies[c]:
            copy.wait()


def pack_left_kernel(seed_hbm, out_ref, seed_ref, sem):
    count, _, rows = seed_ref.shape
    copy = pltpu.make_async_copy(seed_hbm.at[:, pl.ds(0, T), :], seed_ref, sem)
    copy.start()
    start, end = count * HALO, out_ref.shape[0]
    out_ref[start:end, :] = jnp.zeros((end - start, rows), jnp.float32)
    copy.wait()

    def body(lb, _):
        out_ref[pl.ds(lb * HALO, HALO), :] = seed_ref[lb, 0:HALO, :]
        return 0

    lax.fori_loop(0, count, body, 0, unroll=15)


def main_kernel(
    g_ref, m_ref, adv_hbm, seed_hbm, w_in, ap_in, f_ref, area_ref, n_ref,
    next_hbm, adj_hbm, scale_ref, s_last, gain_ref, loss_ref, w_ref,
    s_buf, p_buf, a_buf, seed_ref, next_buf, adj_buf, f_buf, area_buf, sems, in_sems,
):
    count, rows = scale_ref.shape[1:]
    levels, columns, _ = f_ref.shape
    bins = count // levels
    peers = g_ref.shape[0]
    tiles = columns // T
    last = columns - T
    chunks = 4
    per = levels // chunks
    copies_in = []
    for c in range(chunks):
        span = pl.ds(c * per * bins, per * bins)
        copies_in.append(
            (
                pltpu.make_async_copy(adv_hbm.at[span], a_buf.at[span], in_sems.at[0, c]),
                pltpu.make_async_copy(seed_hbm.at[span], seed_ref.at[span], in_sems.at[1, c]),
            )
        )
        copies_in[c][0].start()
        copies_in[c][1].start()
    ones = jnp.ones((peers, rows), jnp.float32)
    sums = [
        lax.dot_general(
            g_ref[:, k, :], ones, (((0,), (0,)), ((), ())), precision=HIGHEST, preferred_element_type=jnp.float32
        )
        for k in range(3)
    ]
    mass_before, mass_after, seed_dot = sums
    direct = seed_dot / mass_after
    rescale = mass_before / mass_after
    scale_ref[0] = rescale
    scale_ref[1] = rescale * direct
    scale_ref[2] = direct

    f_row = count * HALO
    area_row = f_row + HALO * levels
    area_buf[0:T, :] = area_ref[last:columns, :]
    area_buf[T : 2 * T, :] = m_ref[area_row : area_row + T, :]

    def copies(c):
        span = pl.ds(c * per * bins, per * bins)
        return (
            pltpu.make_async_copy(next_buf.at[span], next_hbm.at[span], sems.at[0, c]),
            pltpu.make_async_copy(adj_buf.at[span], adj_hbm.at[span, pl.ds(0, last), :], sems.at[1, c]),
        )

    def level_body(level, _):
        shift_is = masks(n_ref, level)
        f_buf[level, 0:T, :] = f_ref[level, last:columns, :]
        f_buf[level, T : 2 * T, :] = m_ref[pl.ds(f_row + HALO * level, T), :]
        cell = T - OFF
        face = pick(lambda r: f_buf[level, pl.ds(r, T), :], cell, shift_is)
        west = pick(lambda r: f_buf[level, pl.ds(r, T), :], cell - 1, shift_is)
        area = pick(lambda r: area_buf[pl.ds(r, T), :], cell, shift_is)
        for k, value in enumerate(tap_weights(face, west, 1.0 / area, shift_is)):
            w_ref[level, k, columns : columns + T, :] = value
        areas = [ap_in[level, T * v : T * v + T, :] for v in range(tiles)]

        def seed_body(b, _):
            lb = level * bins + b
            rescale = scale_ref[0, pl.ds(lb, 1), :]
            feedback = scale_ref[1, pl.ds(lb, 1), :]
            for v in range(tiles):
                positive, ratio = floor_parts(a_buf[lb, T * v : T * v + T, :])
                p_buf[b, T * v : T * v + T, :] = positive
                seed = seed_ref[lb, T * v : T * v + T, :]
                value = (rescale * seed - feedback * areas[v]) * ratio
                s_buf[b, T * v : T * v + T, :] = value
                if v == tiles - 1:
                    s_last[lb, 0:T, :] = value
            positive, ratio = floor_parts(m_ref[pl.ds(lb * HALO, T), :])
            p_buf[b, columns : columns + T, :] = positive
            gain_ref[lb] = rescale * ratio
            loss_ref[lb] = (feedback * area) * ratio
            return 0

        lax.fori_loop(0, bins, seed_body, 0, unroll=True)
        weights = [
            [w_ref[level, k, pl.ds(T * q + OFF + LEFT - k, T), :] for k in range(LEFT + RIGHT + 1)]
            for q in range(tiles - 1)
        ]

        def bin_body(b, _):
            lb = level * bins + b
            rescale = scale_ref[0, pl.ds(lb, 1), :]
            direct = scale_ref[2, pl.ds(lb, 1), :]
            for q in range(tiles):
                if q < tiles - 1:
                    total = area_ref[T * q : T * q + T, :] * direct
                    for k in range(LEFT + RIGHT + 1):
                        total = total + weights[q][k] * s_buf[b, pl.ds(T * q + OFF + LEFT - k, T), :]
                    adj_buf[lb, T * q : T * q + T, :] = total
                positive = pick_back(lambda r: p_buf[b, pl.ds(r, T), :], T * q + OFF, shift_is)
                next_buf[lb, T * q : T * q + T, :] = positive * rescale
            return 0

        lax.fori_loop(0, bins, bin_body, 0, unroll=True)
        return 0

    for c in range(chunks):
        copies_in[c][0].wait()
        copies_in[c][1].wait()
        lax.fori_loop(c * per, (c + 1) * per, level_body, 0)
        for copy in copies(c):
            copy.start()
    for c in range(chunks):
        for copy in copies(c):
            copy.wait()


def right_kernel(
    m_ref, gain_ref, loss_ref, s_in, w_ref, scale_ref, area_ref, adj_in,
    adj_hbm, s_ref,
    adj_buf, sems,
):
    count = adj_buf.shape[0]
    levels = w_ref.shape[0]
    bins = count // levels
    columns = area_ref.shape[0]
    last = columns - T
    parts = in_chunks(levels, sems.shape[0])

    def copy_of(c):
        span = pl.ds(parts[c][0] * bins, (parts[c][1] - parts[c][0]) * bins)
        return pltpu.make_async_copy(adj_buf.at[span], adj_hbm.at[span, pl.ds(last, T), :], sems.at[c])

    def level_body(level, _):
        for b in range(bins):
            lb = level * bins + b
            s_ref[lb, T : 2 * T, :] = gain_ref[lb] * m_ref[pl.ds(lb * HALO, T), :] - loss_ref[lb]
        weights = [w_ref[level, k, pl.ds(last + OFF + LEFT - k, T), :] for k in range(LEFT + RIGHT + 1)]
        area = area_ref[last:columns, :]
        for b in range(bins):
            lb = level * bins + b
            total = area * scale_ref[2, pl.ds(lb, 1), :]
            for k in range(LEFT + RIGHT + 1):
                total = total + weights[k] * s_ref[lb, pl.ds(OFF + LEFT - k, T), :]
            adj_buf[lb] = total
        return 0

    for c, (start, end) in enumerate(parts):
        lax.fori_loop(start, end, level_body, 0)
        copy_of(c).start()
    for c in range(len(parts)):
        copy_of(c).wait()


def padded(rows):
    return (rows + 2 * T - 1) // T * T


def shards(tracer, courant_frac, departure_shift, cell_area, adjoint_seed):
    levels, bins, columns, rows = tracer.shape
    count = levels * bins
    f32 = jnp.float32
    tile = lax.axis_size("tile")
    to_right = [(i, (i + 1) % tile) for i in range(tile)]
    to_left = [(target, source) for source, target in to_right]
    hbm = pl.BlockSpec(memory_space=pl.ANY)
    vmem = pl.BlockSpec(memory_space=pltpu.VMEM)
    params = pltpu.CompilerParams(vmem_limit_bytes=VMEM_LIMIT)
    dma = pltpu.SemaphoreType.DMA
    taps = LEFT + RIGHT + 1

    def held(x):
        return pltpu.with_memory_space_constraint(x, pltpu.VMEM)

    def far(x):
        return pltpu.with_memory_space_constraint(x, pltpu.HBM)

    def cost(flops, nbytes):
        return pl.CostEstimate(flops=flops, bytes_accessed=nbytes, transcendentals=0)

    size = 4 * count * columns * rows
    t = tracer.reshape(count, columns, rows)
    seed = adjoint_seed.reshape(count, columns, rows)

    message = pl.pallas_call(
        pack_right_kernel,
        out_shape=jax.ShapeDtypeStruct((padded(T + count * (HALO + MAXOFF) + LEFT * levels + MAXOFF), rows), f32),
        in_specs=[hbm] * 5,
        out_specs=vmem,
        scratch_shapes=[
            pltpu.VMEM((count, T, rows), f32),
            pltpu.VMEM((count, T, rows), f32),
            pltpu.VMEM((levels, T, rows), f32),
            pltpu.VMEM((T, rows), f32),
            pltpu.VMEM((levels, rows), jnp.int32),
            dma((2, 4)),
            dma((3,)),
        ],
        compiler_params=params,
        cost_estimate=cost(0, size),
        name="pack_right",
    )(far(t), far(seed), far(courant_frac), far(cell_area), far(departure_shift))
    from_left = lax.ppermute(message, "tile", to_right)

    t0, s0, adv, seeds, w, ap, red = pl.pallas_call(
        interior_kernel,
        out_shape=(
            pltpu.VMEM((count, 2 * T, rows), f32),
            pltpu.VMEM((count, T, rows), f32),
            pltpu.HBM((count, columns, rows), f32),
            pltpu.HBM((count, columns, rows), f32),
            pltpu.VMEM((levels, taps, columns + T, rows), f32),
            pltpu.VMEM((levels, columns + T, rows), f32),
            pltpu.VMEM((3, count, rows), f32),
        ),
        in_specs=[hbm, hbm, vmem, vmem, vmem],
        out_specs=(vmem, vmem, hbm, hbm, vmem, vmem, vmem),
        scratch_shapes=[
            pltpu.VMEM((count, columns, rows), f32),
            pltpu.VMEM((count, columns, rows), f32),
            pltpu.VMEM((count, columns - T, rows), f32),
            pltpu.VMEM((count, columns - T, rows), f32),
            pltpu.VMEM((3, count * T, rows), f32),
            dma((2, 4)),
            dma((2, 4)),
        ],
        compiler_params=params,
        cost_estimate=cost(30 * size, 4 * size),
        name="interior",
    )(far(t), far(seed), courant_frac, cell_area, departure_shift)

    _, w, ap, adv, seeds, sums, adv_left = pl.pallas_call(
        left_kernel,
        out_shape=(
            pltpu.VMEM(t0.shape, f32),
            pltpu.VMEM(w.shape, f32),
            pltpu.VMEM(ap.shape, f32),
            pltpu.HBM(adv.shape, f32),
            pltpu.HBM(seeds.shape, f32),
            jax.ShapeDtypeStruct((tile, 3, count), f32),
            jax.ShapeDtypeStruct((padded(count * HALO + HALO * levels + HALO), rows), f32),
        ),
        in_specs=[vmem] * 5 + [hbm] * 2 + [vmem] * 4,
        out_specs=(vmem,) * 3 + (hbm,) * 2 + (vmem,) * 2,
        input_output_aliases={1: 0, 3: 1, 4: 2, 5: 3, 6: 4},
        scratch_shapes=[
            pltpu.VMEM((count, T, rows), f32),
            pltpu.VMEM((count, T, rows), f32),
            pltpu.VMEM((2, count * T, rows), f32),
            pltpu.VMEM((2, count, rows), f32),
            pltpu.VMEM((levels, 2 * T, rows), f32),
            pltpu.VMEM((2 * T, rows), f32),
            dma((2, 4)),
        ],
        compiler_params=params,
        cost_estimate=cost(10 * size, size),
        name="left_edge",
    )(
        from_left, held(t0), held(s0), held(w), held(ap), far(adv), far(seeds), held(red),
        courant_frac, cell_area, departure_shift,
    )

    adv_right = lax.ppermute(adv_left, "tile", to_left)
    sums = lax.all_to_all(sums, "tile", 0, 0)
    seed_left = pl.pallas_call(
        pack_left_kernel,
        out_shape=jax.ShapeDtypeStruct((padded(count * HALO), rows), f32),
        in_specs=[hbm],
        out_specs=vmem,
        scratch_shapes=[pltpu.VMEM((count, T, rows), f32), dma],
        compiler_params=params,
        cost_estimate=cost(size, size),
        name="pack_left",
    )(far(seeds))
    seed_right = lax.ppermute(seed_left, "tile", to_left)

    tracer_next, tracer_adjoint, scale, s_last, gain, loss, w = pl.pallas_call(
        main_kernel,
        out_shape=(
            jax.ShapeDtypeStruct((count, columns, rows), f32),
            jax.ShapeDtypeStruct((count, columns, rows), f32),
            pltpu.VMEM((3, count, rows), f32),
            pltpu.VMEM((count, 2 * T, rows), f32),
            pltpu.VMEM((count, T, rows), f32),
            pltpu.VMEM((count, T, rows), f32),
            pltpu.VMEM(w.shape, f32),
        ),
        in_specs=[vmem] * 2 + [hbm] * 2 + [vmem] * 5,
        out_specs=(hbm, hbm) + (vmem,) * 5,
        input_output_aliases={4: 6},
        scratch_shapes=[
            pltpu.VMEM((bins, columns, rows), f32),
            pltpu.VMEM((bins, columns + T, rows), f32),
            pltpu.VMEM((count, columns, rows), f32),
            pltpu.VMEM((count, columns, rows), f32),
            pltpu.VMEM((count, columns, rows), f32),
            pltpu.VMEM((count, columns - T, rows), f32),
            pltpu.VMEM((levels, 2 * T, rows), f32),
            pltpu.VMEM((2 * T, rows), f32),
            dma((2, 4)),
            dma((2, 4)),
        ],
        compiler_params=params,
        cost_estimate=cost(MAIN_FLOPS * size, 4 * size),
        name="main_part",
    )(
        sums, adv_right, far(adv), far(seeds), held(w), held(ap),
        courant_frac, cell_area, departure_shift,
    )

    tracer_adjoint, _ = pl.pallas_call(
        right_kernel,
        out_shape=(jax.ShapeDtypeStruct((count, columns, rows), f32), pltpu.VMEM(s_last.shape, f32)),
        in_specs=[vmem] * 7 + [hbm],
        out_specs=(hbm, vmem),
        input_output_aliases={7: 0, 3: 1},
        scratch_shapes=[pltpu.VMEM((count, T, rows), f32), dma((4,))],
        compiler_params=params,
        cost_estimate=cost(10 * size, size),
        name="right_edge",
    )(seed_right, held(gain), held(loss), held(s_last), held(w), held(scale), cell_area, tracer_adjoint)
    return tracer_next.reshape(tracer.shape), tracer_adjoint.reshape(tracer.shape)


def solution(mesh):
    return jax.shard_map(
        shards,
        mesh=mesh,
        in_specs=(
            P("group", None, "tile", None),
            P("group", "tile", None),
            P("group", None),
            P("tile", None),
            P("group", None, "tile", None),
        ),
        out_specs=(P("group", None, "tile", None), P("group", None, "tile", None)),
        check_vma=False,
    )
```

time: 52.4 us -> 42.2 us (0.81)
  blocking collectives: 15.5 us -> 0 us
  starting transfers between devices: 0.51 us -> 8.78 us
  local copies, waits for them, and re-layouts: 5.3 us -> 0.01 us
  waiting for transfers between devices: 12.1 us -> 13.3 us
  Pallas kernels: 18.1 us -> 19.1 us
    all_to_all x1 -> x0, blocking collectives: 15.5 us -> none  [shards(): sums = lax.all_to_all(sums, 'tile', 0, 0)]
    unnamed x10 -> x6, local copies, waits for them, and re-layouts: 5.3 us -> 0.01 us
    ppermute x2 -> x3, starting transfers between devices: 0.51 us -> 5 us  [the longest x1 4.43 us: shards(): seed_right = lax.ppermute(seed_left, 'tile', to_left)]
    pallas_call x3 -> x4, Pallas kernels: 6.89 us -> 11.1 us  [the longest x1 4.75 us: shards(): pl.pallas_call(interior_kernel, out_shape=(pltpu.VMEM((count, 2 * T, rows...]
    pallas_call x1, Pallas kernels: 5.47 us -> 1.52 us  [shards(): pl.pallas_call(right_kernel, out_shape=(jax.ShapeDtypeStruct((count, colu...]
    all_to_all x0 -> x1, starting transfers between devices: none -> 3.78 us  [shards(): sums = lax.all_to_all(sums, 'tile', 0, 0)]
    all_to_all x0 -> x1, waiting for transfers between devices: none -> 2.18 us  [shards(): sums = lax.all_to_all(sums, 'tile', 0, 0)]
    ppermute x2 -> x3, waiting for transfers between devices: 12.1 us -> 11.1 us  [the longest x1 11.1 us: shards(): from_left = lax.ppermute(message, 'tile', to_right)]
  transfers between devices with their start and end apart: 2 -> 4, of which waited for: 1 -> 2; matrix products, arithmetic and copies ran while one was open for 0% -> 0% of each run, Pallas kernels for 23% -> 30%
where the time goes in v2:
time: 42.2 us; the launch traced here: 41.9 us
  Pallas kernels  19.1 us (45%)
  waiting for transfers between devices  13.3 us (32%)
  starting transfers between devices  8.78 us (21%)
  between operations  0.72 us (2%)
    ppermute x1, waiting for transfers between devices, shards(): from_left = lax.ppermute(message, 'tile', to_right)  11.1 us
    pallas_call x1, Pallas kernels, shards(): pl.pallas_call(main_kernel, out_shape=(jax.ShapeDtypeStruct((count, colum...  6.47 us
    pallas_call x1, Pallas kernels, shards(): pl.pallas_call(interior_kernel, out_shape=(pltpu.VMEM((count, 2 * T, rows...  4.75 us
    ppermute x1, starting transfers between devices, shards(): seed_right = lax.ppermute(seed_left, 'tile', to_left)  4.43 us
    all_to_all x1, starting transfers between devices, shards(): sums = lax.all_to_all(sums, 'tile', 0, 0)  3.78 us
    pallas_call x1, Pallas kernels, shards(): pl.pallas_call(left_kernel, out_shape=(pltpu.VMEM(t0.shape, f32), pltpu.V...  3.15 us
    all_to_all x1, waiting for transfers between devices, shards(): sums = lax.all_to_all(sums, 'tile', 0, 0)  2.18 us
    pallas_call x1, Pallas kernels, shards(): pl.pallas_call(pack_right_kernel, out_shape=jax.ShapeDtypeStruct((padded(...  1.88 us
  transfers between devices with their start and end apart: 4, of which 2 were waited for; matrix products, arithmetic and copies ran while one was open for 0% of the time, Pallas kernels for 30%

profile of v2, /device:TPU:0, one launch (start us, length us, event | category | flops | bytes accessed | tf_op | source)
XLA Modules:
  0.0 41.9 jit_solution(3244373213792181144)
XLA Ops:
  0.6 0.0 copy-start
  0.6 0.0 copy-start.1
  0.7 0.0 copy-start.2
  0.7 1.9 %pack_right.1 = f32[1752,128]{1,0:T(8,128)S(1)} custom-call(f32[240,24,128]{2,1,0:T(8,128)} %bitcast.4, f32[240,24,128]{2,1,0:T(8,128)} %bitcast.6, f32[16,24,128]{2,1,0:T(8,128)} %f_ref.5, f32[24,128]{1,0:T(8,128)} %area_ref.7, s32[16,128]{1,0:T(8,128)} %n_ref.5), custom_call_target="tpu_custom_call" | custom-call | bytes 2949120 | tf_op jit(solution)/shard_map/pack_right/pallas_call | solution.py:521
  2.5 0.5 %collective-permute-start = (f32[1752,128]{1,0:T(8,128)S(1)}, f32[1752,128]{1,0:T(8,128)S(1)}, u32[]{:S(2)}, u32[]{:S(2)}) collective-permute-start(f32[1752,128]{1,0:T(8,128)S(1)} %pack_right.1), channel_id=1, source_target_pairs={{0,1},{1,2},{2,3},{3,4},{4,5},{5,6},{6,7},{7,8},{8,9},{9,10},{10,1... | collective-permute-start | bytes 2691080 | tf_op jit(solution)/shard_map/ppermute | solution.py:539
  3.1 0.0 copy-done
  3.1 0.0 copy-done.1
  3.1 0.0 copy-done.2
  3.1 4.8 %interior.1 = (f32[240,16,128]{2,1,0:T(8,128)S(1)}, f32[240,8,128]{2,1,0:T(8,128)S(1)}, f32[240,24,128]{2,1,0:T(8,128)}, f32[240,24,128]{2,1,0:T(8,128)}, f32[16...) custom-call(f32[240,24,128]{2,1,0:T(8,128)} %bitcast.5, f32[240,24,128]{2,1,0:T(8,128)} %bitcast.7, ...), custom_call_target="tpu_custom_call" | custom-call | flops 88473600 | bytes 11796480 | tf_op jit(solution)/shard_map/interior/pallas_call | solution.py:541
  7.8 11.1 %collective-permute-done.m_ref = f32[1752,128]{1,0:T(8,128)S(1)} collective-permute-done((f32[1752,128]{1,0:T(8,128)S(1)}, f32[1752,128]{1,0:T(8,128)S(1)}, u32[]{:S(2)}, u32[]{:S(2)}) %collective-permute-start) | collective-permute-done | bytes 897056 | tf_op jit(solution)/shard_map/ppermute | solution.py:539
  18.9 3.1 %left_edge.1 = (f32[240,16,128]{2,1,0:T(8,128)S(1)}, f32[16,6,32,128]{3,2,1,0:T(8,128)S(1)}, f32[16,32,128]{2,1,0:T(8,128)S(1)}, f32[240,24,128]{2,1,0:T(8,128)}...) custom-call(f32[1752,128]{1,0:T(8,128)S(1)} %collective-permute-done, ...), custom_call_target="tpu_custom_call", output_to_operand_aliasing={{0}: (1, {}), {1}: (3, {}), {2}: (4, {}), {3}: (5, {}), {4}... | custom-call | flops 29491200 | bytes 2949120 | tf_op jit(solution)/shard_map/left_edge/pallas_call | solution.py:568
  22.1 0.1 collective-permute-start.1
  22.1 3.8 %all-to-all-start = ((f32[16,3,240]{2,1,0:T(4,128)}), f32[16,3,240]{2,1,0:T(4,128)S(1)}, u32[]{:S(2)}, u32[]{:S(2)}) async-start(f32[16,3,240]{2,1,0:T(4,128)} %get-tuple-element.30), calls=%async_computation | async-start | bytes 131072 | tf_op jit(solution)/shard_map/all_to_all | solution.py:600
  25.9 1.4 %pack_left.1 = f32[1208,128]{1,0:T(8,128)S(1)} custom-call(f32[240,24,128]{2,1,0:T(8,128)} %get-tuple-element.33.seed_hbm), custom_call_target="tpu_custom_call" | custom-call | flops 2949120 | bytes 2949120 | tf_op jit(solution)/shard_map/pack_left/pallas_call | solution.py:601
  27.3 4.4 %collective-permute-start.2 = (f32[1208,128]{1,0:T(8,128)S(1)}, f32[1208,128]{1,0:T(8,128)S(1)}, u32[]{:S(2)}, u32[]{:S(2)}) collective-permute-start(f32[1208,128]{1,0:T(8,128)S(1)} %pack_left.1), channel_id=1, source_target_pairs={{1,0},{2,1},{3,2},{4,3},{5,4},{6,5},{7,6},{8,7},{9,8},{10,9},{11,1... | collective-permute-start | bytes 1855496 | tf_op jit(solution)/shard_map/ppermute | solution.py:611
  31.7 2.2 %all-to-all-done.g_ref = f32[16,3,240]{2,1,0:T(4,128)S(1)} async-done(((f32[16,3,240]{2,1,0:T(4,128)}), f32[16,3,240]{2,1,0:T(4,128)S(1)}, u32[]{:S(2)}, u32[]{:S(2)}) %all-to-all-start) | async-done | bytes 46112 | tf_op jit(solution)/shard_map/all_to_all | solution.py:600
  33.9 0.0 collective-permute-done.1.m_ref
  33.9 6.5 %main_part.1 = (f32[240,24,128]{2,1,0:T(8,128)}, f32[240,24,128]{2,1,0:T(8,128)}, f32[3,240,128]{2,1,0:T(8,128)S(1)}, f32[240,16,128]{2,1,0:T(8,128)S(1)}, f32[2...) custom-call(f32[16,3,240]{2,1,0:T(4,128)S(1)} %all-to-all-done.g_ref, ...), custom_call_target="tpu_custom_call", output_to_operand_aliasing={{6}: (4, {})} | custom-call | flops 8847360000 | bytes 11796480 | tf_op jit(solution)/shard_map/main_part/pallas_call | solution.py:613
  40.4 0.0 collective-permute-done.2.m_ref
  40.4 1.5 %right_edge.1 = (f32[240,24,128]{2,1,0:T(8,128)}, f32[240,16,128]{2,1,0:T(8,128)S(1)}) custom-call(f32[1208,128]{1,0:T(8,128)S(1)} %collective-permute-done.2.m_ref, f32[240,8,128]{2,1,0:T(8,128)S(1)} %get-tuple-element.37.gain_ref, f32[240,8,128]{2,1,0:T(8,128)S(1)} %get-tuple-element.38.loss_ref, ...), custom_call_target="tpu_custom_call", output_to_operand_aliasing={{0}: (7, {}), {1}: (3, {})} | custom-call | flops 29491200 | bytes 2949120 | tf_op jit(solution)/shard_map/right_edge/pallas_call | solution.py:647
Async XLA Ops:
  0.6 2.4 %copy-start = (f32[16,24,128]{2,1,0:T(8,128)S(1)}, f32[16,24,128]{2,1,0:T(8,128)}, u32[]{:S(2)}) copy-start(f32[16,24,128]{2,1,0:T(8,128)} %f_ref.5) | copy-start | bytes 589828
  0.6 2.4 %copy-start.1 = (f32[24,128]{1,0:T(8,128)S(1)}, f32[24,128]{1,0:T(8,128)}, u32[]{:S(2)}) copy-start(f32[24,128]{1,0:T(8,128)} %area_ref.7) | copy-start | bytes 36868
  0.7 2.4 %copy-start.2 = (s32[16,128]{1,0:T(8,128)S(1)}, s32[16,128]{1,0:T(8,128)}, u32[]{:S(2)}) copy-start(s32[16,128]{1,0:T(8,128)} %n_ref.5) | copy-start | bytes 24580
  2.5 16.4 %collective-permute-start = (f32[1752,128]{1,0:T(8,128)S(1)}, f32[1752,128]{1,0:T(8,128)S(1)}, u32[]{:S(2)}, u32[]{:S(2)}) collective-permute-start(f32[1752,128]{1,0:T(8,128)S(1)} %pack_right.1), channel_id=1, source_target_pairs={{0,1},{1,2},{2,3},{3,4},{4,5},{5,6},{6,7},{7,8},{8,9},{9,10},{10,1... | collective-permute-start | bytes 2691080 | tf_op jit(solution)/shard_map/ppermute | solution.py:539
  22.1 11.8 %collective-permute-start.1 = (f32[1296,128]{1,0:T(8,128)}, f32[1296,128]{1,0:T(8,128)}, u32[]{:S(2)}, u32[]{:S(2)}) collective-permute-start(f32[1296,128]{1,0:T(8,128)} %get-tuple-element.31), channel_id=1, source_target_pairs={{1,0},{2,1},{3,2},{4,3},{5,4},{6,5},{7,6},{8,7},{9,8},{10,9},{11,1... | collective-permute-start | bytes 1990664 | tf_op jit(solution)/shard_map/ppermute | solution.py:599
  22.1 11.8 %all-to-all-start = ((f32[16,3,240]{2,1,0:T(4,128)}), f32[16,3,240]{2,1,0:T(4,128)S(1)}, u32[]{:S(2)}, u32[]{:S(2)}) async-start(f32[16,3,240]{2,1,0:T(4,128)} %get-tuple-element.30), calls=%async_computation | async-start | bytes 131072 | tf_op jit(solution)/shard_map/all_to_all | solution.py:600
  27.3 13.1 %collective-permute-start.2 = (f32[1208,128]{1,0:T(8,128)S(1)}, f32[1208,128]{1,0:T(8,128)S(1)}, u32[]{:S(2)}, u32[]{:S(2)}) collective-permute-start(f32[1208,128]{1,0:T(8,128)S(1)} %pack_left.1), channel_id=1, source_target_pairs={{1,0},{2,1},{3,2},{4,3},{5,4},{6,5},{7,6},{8,7},{9,8},{10,9},{11,1... | collective-permute-start | bytes 1855496 | tf_op jit(solution)/shard_map/ppermute | solution.py:611

commit v3 on v2

v3 whole, which is shorter than its diff:
```python
import jax
import jax.numpy as jnp
from jax import lax
from jax.experimental import pallas as pl
from jax.experimental.pallas import tpu as pltpu
from jax.sharding import PartitionSpec as P

MAXOFF = 2
FLOOR2 = 0.1 * 0.1
LEFT, RIGHT = 3, 2
OFF = MAXOFF
HALO = LEFT + MAXOFF
T = 8
LANES = 128
VMEM_LIMIT = 20 * 2**20
CHUNKS = 8
HIGHEST = lax.Precision.HIGHEST


def tap_weights(face, west, inverse, shift_is):
    def taps(f):
        f2 = f * f
        f3 = f2 * f
        alpha = 3.0 * f2 - 2.0 * f3
        beta = f3 - f2
        gamma = f - 2.0 * f2 + f3
        return (
            beta * (-1.0 / 12.0),
            (7.0 / 12.0) * beta - (1.0 / 12.0) * gamma,
            alpha + (7.0 / 12.0) * (beta + gamma),
            (7.0 / 12.0) * gamma - (1.0 / 12.0) * beta,
            gamma * (-1.0 / 12.0),
        )

    east_taps, west_taps = taps(face), taps(west)
    weights = [west_taps[0] * inverse]
    for k in range(4):
        weights.append((west_taps[k + 1] - east_taps[k]) * inverse)
    weights.append(-east_taps[4] * inverse)
    is0, is1, is2 = shift_is
    rest = 1.0 - inverse
    weights[3] = weights[3] + jnp.where(is0, 1.0, inverse)
    weights[4] = weights[4] + jnp.where(is1, rest, 0.0)
    weights[5] = weights[5] + jnp.where(is2, rest, 0.0)
    return weights


def masks(shift_ref, level):
    n = jnp.broadcast_to(shift_ref[pl.ds(level, 1), :], (T, shift_ref.shape[1]))
    return n == 0, n == 1, n == 2


def pick(load, start, shift_is):
    return jnp.where(
        shift_is[0], load(start), jnp.where(shift_is[1], load(start + 1), load(start + 2))
    )


def pick_back(load, start, shift_is):
    return jnp.where(
        shift_is[0], load(start), jnp.where(shift_is[1], load(start - 1), load(start - 2))
    )


def pick_first(load, shift_is):
    first = load(0)
    two_down = jnp.concatenate([first[T - 2 : T], first[0 : T - 2]], axis=0)
    one_down = jnp.concatenate([first[T - 1 : T], first[0 : T - 1]], axis=0)
    return jnp.where(shift_is[0], two_down, jnp.where(shift_is[1], one_down, first))


def pick_last(load, shift_is):
    first = load(0)
    two_up = jnp.concatenate([first[T - 2 : T], first[0 : T - 2]], axis=0)
    one_up = jnp.concatenate([first[T - 1 : T], first[0 : T - 1]], axis=0)
    return jnp.where(shift_is[0], two_up, one_up)


def fir(weights, load, start):
    total = weights[0] * load(start)
    for k in range(1, LEFT + RIGHT + 1):
        total = total + weights[k] * load(start + k)
    return total


def floor_parts(advected):
    square = advected * advected + FLOOR2
    root = lax.rsqrt(square)
    return square * root, advected * root


def pack_right_kernel(t_hbm, s_hbm, f_hbm, area_hbm, n_hbm, out_ref, t_buf, s_buf, f_buf, area_buf, n_buf, sems, small):
    count, columns, rows = t_hbm.shape
    levels = f_hbm.shape[0]
    bins = count // levels
    chunks = sems.shape[1]
    per = levels // chunks
    t_rows, s_rows = t_buf.shape[1], s_buf.shape[1]

    def copies(c):
        span = pl.ds(c * per * bins, per * bins)
        return (
            pltpu.make_async_copy(t_hbm.at[span, pl.ds(columns - t_rows, t_rows), :], t_buf.at[span], sems.at[0, c]),
            pltpu.make_async_copy(s_hbm.at[span, pl.ds(columns - s_rows, s_rows), :], s_buf.at[span], sems.at[1, c]),
        )

    others = [
        pltpu.make_async_copy(n_hbm, n_buf, small.at[0]),
        pltpu.make_async_copy(f_hbm.at[:, pl.ds(columns - T, T), :], f_buf, small.at[1]),
        pltpu.make_async_copy(area_hbm.at[pl.ds(columns - T, T), :], area_buf, small.at[2]),
    ]
    others[0].start()
    for c in range(chunks):
        for copy in copies(c):
            copy.start()
    for copy in others[1:]:
        copy.start()
    width = HALO + MAXOFF
    end = out_ref.shape[0]
    row = T + count * width
    last = row + LEFT * levels
    out_ref[0:T, :] = jnp.zeros((T, rows), jnp.float32)
    out_ref[last + MAXOFF : end, :] = jnp.zeros((end - last - MAXOFF, rows), jnp.float32)
    others[0].wait()

    def level_body(level, _):
        @pl.when(level % per == 0)
        def _():
            for copy in copies(level // per):
                copy.wait()

        unshifted = n_buf[pl.ds(level, 1), :] == 0

        def bin_body(b, _):
            lb = level * bins + b
            row = T + lb * width
            out_ref[pl.ds(row, HALO), :] = t_buf[lb, t_rows - HALO : t_rows, :]
            second = s_buf[lb, s_rows - 1 : s_rows, :]
            out_ref[pl.ds(row + HALO, 1), :] = jnp.where(unshifted, s_buf[lb, s_rows - 2 : s_rows - 1, :], second)
            out_ref[pl.ds(row + HALO + 1, 1), :] = second
            return 0

        lax.fori_loop(0, bins, bin_body, 0, unroll=15)
        return 0

    lax.fori_loop(0, levels, level_body, 0)
    for copy in others[1:]:
        copy.wait()
    for level in range(levels):
        out_ref[row + LEFT * level : row + LEFT * (level + 1), :] = f_buf[level, T - LEFT : T, :]
    out_ref[last : last + MAXOFF, :] = area_buf[T - MAXOFF : T, :]


def shifted_weights(f_of, area_of, cell, shift_is):
    face = pick(f_of, cell, shift_is)
    west = pick(f_of, cell - 1, shift_is)
    area = pick(area_of, cell, shift_is)
    return area, tap_weights(face, west, 1.0 / area, shift_is)


def each_chunk(level, per, act):
    @pl.when(level % per == 0)
    def _():
        act(level // per)


def interior_kernel(
    t_hbm, s_hbm, f_ref, area_ref, n_ref,
    t0_ref, s0_ref, t2_ref, s2_ref, ratio_ref, pos_ref, seed_ref, w_ref, ap_ref, red_ref, out_ref,
    t_buf, s_buf, part, in_sems,
):
    count, columns, rows = t_hbm.shape
    levels = f_ref.shape[0]
    bins = count // levels
    chunks = in_sems.shape[1]
    per = levels // chunks
    tiles = range(1, columns // T)
    last = columns - T
    width = 2 * HALO

    def copies_in(c):
        span = pl.ds(c * per * bins, per * bins)
        return (
            pltpu.make_async_copy(t_hbm.at[span], t_buf.at[span], in_sems.at[0, c]),
            pltpu.make_async_copy(s_hbm.at[span], s_buf.at[span], in_sems.at[1, c]),
        )

    for c in range(chunks):
        for copy in copies_in(c):
            copy.start()
    row = count * width
    for level in range(levels):
        out_ref[row + HALO * level : row + HALO * (level + 1), :] = f_ref[level, 0:HALO, :]
    row = row + HALO * levels
    out_ref[row : row + HALO, :] = area_ref[0:HALO, :]
    end = out_ref.shape[0]
    out_ref[row + HALO : end, :] = jnp.zeros((end - row - HALO, rows), jnp.float32)

    def level_body(level, _):
        def arrive(c):
            for copy in copies_in(c):
                copy.wait()

        each_chunk(level, per, arrive)
        shift_is = masks(n_ref, level)
        own = []
        for v in tiles:
            area, w = shifted_weights(
                lambda r: f_ref[level, pl.ds(r, T), :], lambda r: area_ref[pl.ds(r, T), :], T * v - OFF, shift_is
            )
            own.append((area, w))
            ap_ref[level, T * v : T * v + T, :] = area
            for k, value in enumerate(w):
                w_ref[level, k, T * v : T * v + T, :] = value
        for b in range(bins):
            lb = level * bins + b
            mass = None
            for v in range(columns // T):
                value = t_buf[lb, T * v : T * v + T, :]
                if v == 0:
                    t0_ref[lb, T : 2 * T, :] = value
                if v == columns // T - 1:
                    t2_ref[lb, 0:T, :] = value
                value = area_ref[T * v : T * v + T, :] * value
                mass = value if mass is None else mass + value
            early = pick_first(lambda r: s_buf[lb, pl.ds(r, T), :], shift_is)
            s0_ref[lb] = early
            s2_ref[lb] = pick_last(lambda r: s_buf[lb, pl.ds(last + r, T), :], shift_is)
            out_ref[pl.ds(lb * width, HALO), :] = t_buf[lb, 0:HALO, :]
            out_ref[pl.ds(lb * width + HALO, HALO), :] = early[0:HALO]
            after = dot = None
            for v, (area, w) in zip(tiles, own):
                cell = T * v - OFF
                advected = fir(w, lambda r: t_buf[lb, pl.ds(r, T), :], cell - LEFT)
                positive, ratio = floor_parts(advected)
                ratio_ref[lb, T * v : T * v + T, :] = ratio
                pos_ref[lb, T * v : T * v + T, :] = positive
                seed = pick(lambda r: s_buf[lb, pl.ds(r, T), :], cell, shift_is)
                seed_ref[lb, T * v : T * v + T, :] = seed
                after = area * positive if after is None else after + area * positive
                dot = seed * positive if dot is None else dot + seed * positive
            for k, value in enumerate((mass, after, dot)):
                part[k, pl.ds(lb * T, T), :] = value
        return 0

    lax.fori_loop(0, levels, level_body, 0)
    reduce_rows(part, red_ref, 3, count)


def reduce_rows(part, red_ref, kinds, count):
    def body(g, _):
        for k in range(kinds):
            total = part[k, pl.ds(g * T * T, T, stride=T), :]
            for s in range(1, T):
                total = total + part[k, pl.ds(g * T * T + s, T, stride=T), :]
            red_ref[k, pl.ds(g * T, T), :] = total
        return 0

    lax.fori_loop(0, count // T, body, 0, unroll=5)
    rest = red_ref.shape[1] - count
    for k in range(kinds):
        red_ref[k, pl.ds(count, rest), :] = jnp.zeros((rest, red_ref.shape[2]), jnp.float32)


def left_kernel(
    m_ref, t0_in, s0_ref, ratio_in, pos_in, seed_in, w_in, ap_in, red_ref, f_ref, area_ref, n_ref,
    t0_ref, ratio_ref, pos_ref, seed_ref, w_ref, ap_ref, sum_ref,
    part, red_new, f_buf, area_buf,
):
    count = t0_ref.shape[0]
    levels, _, rows = f_ref.shape
    bins = count // levels
    width = HALO + MAXOFF
    f_row = T + count * width
    area_row = f_row + LEFT * levels
    area_buf[0:T, :] = m_ref[area_row - (T - MAXOFF) : area_row + MAXOFF, :]
    area_buf[T : 2 * T, :] = area_ref[0:T, :]
    cell = T - OFF
    sublane = lax.broadcasted_iota(jnp.int32, (T, rows), 0)

    def level_body(level, _):
        shift_is = masks(n_ref, level)
        remote = sublane + jnp.broadcast_to(n_ref[pl.ds(level, 1), :], (T, rows)) < OFF
        f_buf[0:T, :] = m_ref[pl.ds(f_row + LEFT * level - (T - LEFT), T), :]
        f_buf[T : 2 * T, :] = f_ref[level, 0:T, :]
        area, w = shifted_weights(
            lambda r: f_buf[pl.ds(r, T), :], lambda r: area_buf[pl.ds(r, T), :], cell, shift_is
        )
        ap_ref[level, 0:T, :] = area
        for k, value in enumerate(w):
            w_ref[level, k, 0:T, :] = value
        for b in range(bins):
            lb = level * bins + b
            t0_ref[lb, 0:T, :] = m_ref[pl.ds(T + lb * width - (T - HALO), T), :]
        for b in range(bins):
            lb = level * bins + b
            advected = fir(w, lambda r: t0_ref[lb, pl.ds(r, T), :], cell - LEFT)
            positive, ratio = floor_parts(advected)
            ratio_ref[lb, 0:T, :] = ratio
            pos_ref[lb, 0:T, :] = positive
            seed = jnp.where(remote, m_ref[pl.ds(T + lb * width + HALO, T), :], s0_ref[lb])
            seed_ref[lb, 0:T, :] = seed
            part[0, pl.ds(lb * T, T), :] = area * positive
            part[1, pl.ds(lb * T, T), :] = seed * positive
        return 0

    lax.fori_loop(0, levels, level_body, 0)
    reduce_rows(part, red_new, 2, count)
    lines = []
    for k in range(3):
        for half in range(2):
            span = pl.ds(half * LANES, LANES)
            values = red_ref[k, span, :]
            if k:
                values = values + red_new[k - 1, span, :]
            lines.append(jnp.sum(values.T, axis=0, keepdims=True))
    lines.append(jnp.zeros((T - len(lines), rows), jnp.float32))
    sum_ref[...] = jnp.broadcast_to(jnp.concatenate(lines, axis=0)[None], sum_ref.shape)


def middle_kernel(
    ratio_ref, pos_in, seed_ref, w_ref, ap_ref, n_ref, sum_in,
    x_ref, y_ref, own_ref, pos_ref, sum_ref,
    x_buf, y_buf,
):
    levels = n_ref.shape[0]
    count = ratio_ref.shape[0]
    bins = count // levels
    tiles = ratio_ref.shape[1] // T
    taps = range(LEFT + RIGHT + 1)

    def level_body(level, _):
        shift_is = masks(n_ref, level)
        areas = [ap_ref[level, T * v : T * v + T, :] for v in range(tiles)]
        for b in range(bins):
            lb = level * bins + b
            for v in range(tiles):
                part = slice(T * v, T * v + T)
                ratio = ratio_ref[lb, part, :]
                x_buf[b, part, :] = seed_ref[lb, part, :] * ratio
                y_buf[b, part, :] = areas[v] * ratio
            x_ref[lb, T * (tiles - 1) : T * tiles, :] = x_buf[b, T * (tiles - 1) : T * tiles, :]
            y_ref[lb, T * (tiles - 1) : T * tiles, :] = y_buf[b, T * (tiles - 1) : T * tiles, :]
        for q in range(tiles - 1):
            weights = [w_ref[level, k, pl.ds(T * q + OFF + LEFT - k, T), :] for k in taps]
            part = slice(T * q, T * q + T)
            for b in range(bins):
                lb = level * bins + b
                for buf, out in ((x_buf, x_ref), (y_buf, y_ref)):
                    total = weights[0] * buf[b, pl.ds(T * q + OFF + LEFT, T), :]
                    for k in taps[1:]:
                        total = total + weights[k] * buf[b, pl.ds(T * q + OFF + LEFT - k, T), :]
                    out[lb, part, :] = total
                own_ref[lb, part, :] = pick_back(lambda r: pos_ref[lb, pl.ds(r, T), :], T * q + OFF, shift_is)
        return 0

    lax.fori_loop(0, levels, level_body, 0)


def final_kernel(
    g_ref, m_ref, t2_in, s2_ref, x_ref, y_ref, own_ref, pos_in, w_ref, f_ref, area_ref, n_ref,
    next_hbm, adj_hbm, t2_ref, pos_ref,
    scale_ref, w_buf, s_buf, next_buf, adj_buf, f_buf, area_buf, out_sems,
):
    count, columns, rows = next_buf.shape
    levels = f_ref.shape[0]
    bins = count // levels
    peers = g_ref.shape[0]
    tiles = columns // T
    last = columns - T
    chunks = out_sems.shape[1]
    per = levels // chunks
    taps = range(LEFT + RIGHT + 1)
    width = 2 * HALO

    def copies_out(c):
        span = pl.ds(c * per * bins, per * bins)
        return (
            pltpu.make_async_copy(next_buf.at[span], next_hbm.at[span], out_sems.at[0, c]),
            pltpu.make_async_copy(adj_buf.at[span], adj_hbm.at[span], out_sems.at[1, c]),
        )

    total = g_ref[0]
    for peer in range(1, peers):
        total = total + g_ref[peer]
    mass_before, mass_after, seed_dot = total[0:2], total[2:4], total[4:6]
    direct = seed_dot / mass_after
    rescale = mass_before / mass_after
    for k, value in enumerate((rescale, rescale * direct, direct)):
        for half in range(2):
            column = jnp.broadcast_to(value[half : half + 1], (LANES, LANES)).T
            scale_ref[k, pl.ds(half * LANES, LANES), :] = column
    f_row = count * width
    area_row = f_row + HALO * levels
    area_buf[0:T, :] = area_ref[last:columns, :]
    area_buf[T : 2 * T, :] = m_ref[area_row : area_row + T, :]
    sublane = lax.broadcasted_iota(jnp.int32, (T, rows), 0)

    def level_body(level, _):
        shift_is = masks(n_ref, level)
        near = sublane + jnp.broadcast_to(n_ref[pl.ds(level, 1), :], (T, rows)) < OFF
        f_buf[0:T, :] = f_ref[level, last:columns, :]
        f_buf[T : 2 * T, :] = m_ref[pl.ds(f_row + HALO * level, T), :]
        area, w = shifted_weights(
            lambda r: f_buf[pl.ds(r, T), :], lambda r: area_buf[pl.ds(r, T), :], T - OFF, shift_is
        )
        for k in taps:
            w_buf[k, 0:T, :] = w_ref[level, k, last:columns, :]
            w_buf[k, T : 2 * T, :] = w[k]
        weights = [w_buf[k, pl.ds(OFF + LEFT - k, T), :] for k in taps]
        for b in range(bins):
            lb = level * bins + b
            t2_ref[lb, T : 2 * T, :] = m_ref[pl.ds(lb * width, T), :]
        for b in range(bins):
            lb = level * bins + b
            rescale = scale_ref[0, pl.ds(lb, 1), :]
            feedback = scale_ref[1, pl.ds(lb, 1), :]
            advected = fir(w, lambda r: t2_ref[lb, pl.ds(r, T), :], T - OFF - LEFT)
            positive, ratio = floor_parts(advected)
            pos_ref[lb, columns : columns + T, :] = positive
            seed = jnp.where(near, s2_ref[lb], m_ref[pl.ds(lb * width + HALO, T), :])
            s_buf[b, 0:T, :] = rescale * x_ref[lb, last:columns, :] - feedback * y_ref[lb, last:columns, :]
            s_buf[b, T : 2 * T, :] = (rescale * seed - feedback * area) * ratio
        for q in range(tiles):
            part = slice(T * q, T * q + T)
            area_own = area_ref[part, :]
            for b in range(bins):
                lb = level * bins + b
                rescale = scale_ref[0, pl.ds(lb, 1), :]
                value = area_own * scale_ref[2, pl.ds(lb, 1), :]
                if q < tiles - 1:
                    value = value + rescale * x_ref[lb, part, :] - scale_ref[1, pl.ds(lb, 1), :] * y_ref[lb, part, :]
                    own = own_ref[lb, part, :]
                else:
                    for k in taps:
                        value = value + weights[k] * s_buf[b, pl.ds(OFF + LEFT - k, T), :]
                    own = pick_back(lambda r: pos_ref[lb, pl.ds(r, T), :], T * q + OFF, shift_is)
                adj_buf[lb, part, :] = value
                next_buf[lb, part, :] = own * rescale

        def leave(c):
            for copy in copies_out(c - 1):
                copy.start()

        each_chunk(level + 1, per, leave)
        return 0

    lax.fori_loop(0, levels, level_body, 0)
    for c in range(chunks):
        for copy in copies_out(c):
            copy.wait()


def padded(rows):
    return (rows + 2 * T - 1) // T * T


def shards(tracer, courant_frac, departure_shift, cell_area, adjoint_seed):
    levels, bins, columns, rows = tracer.shape
    count = levels * bins
    f32 = jnp.float32
    tile = lax.axis_size("tile")
    to_right = [(i, (i + 1) % tile) for i in range(tile)]
    to_left = [(target, source) for source, target in to_right]
    hbm = pl.BlockSpec(memory_space=pl.ANY)
    vmem = pl.BlockSpec(memory_space=pltpu.VMEM)
    params = pltpu.CompilerParams(vmem_limit_bytes=VMEM_LIMIT)
    dma = pltpu.SemaphoreType.DMA
    taps = LEFT + RIGHT + 1

    def held(x):
        return pltpu.with_memory_space_constraint(x, pltpu.VMEM)

    def far(x):
        return pltpu.with_memory_space_constraint(x, pltpu.HBM)

    def cost(flops, nbytes):
        return pl.CostEstimate(flops=flops, bytes_accessed=nbytes, transcendentals=0)

    size = 4 * count * columns * rows
    t = tracer.reshape(count, columns, rows)
    seed = adjoint_seed.reshape(count, columns, rows)

    message = pl.pallas_call(
        pack_right_kernel,
        out_shape=jax.ShapeDtypeStruct((padded(T + count * (HALO + MAXOFF) + LEFT * levels + MAXOFF), rows), f32),
        in_specs=[hbm] * 5,
        out_specs=vmem,
        scratch_shapes=[
            pltpu.VMEM((count, HALO, rows), f32),
            pltpu.VMEM((count, MAXOFF, rows), f32),
            pltpu.VMEM((levels, T, rows), f32),
            pltpu.VMEM((T, rows), f32),
            pltpu.VMEM((levels, rows), jnp.int32),
            dma((2, 2)),
            dma((3,)),
        ],
        compiler_params=params,
        cost_estimate=cost(0, size),
        name="pack_right",
    )(far(t), far(seed), far(courant_frac), far(cell_area), far(departure_shift))
    from_left = lax.ppermute(message, "tile", to_right)

    strip = pltpu.VMEM((count, T, rows), f32)
    two_strips = pltpu.VMEM((count, 2 * T, rows), f32)
    whole = pltpu.VMEM((count, columns, rows), f32)
    wide = pltpu.VMEM((count, columns + T, rows), f32)
    w_shape = pltpu.VMEM((levels, taps, columns, rows), f32)
    ap_shape = pltpu.VMEM((levels, columns, rows), f32)
    left_rows = padded(2 * count * HALO + HALO * levels + HALO)

    t0, s0, t2, s2, ratio, positive, seeds, w, ap, red, message_left = pl.pallas_call(
        interior_kernel,
        out_shape=(
            two_strips, strip, two_strips, strip, whole, wide, whole, w_shape, ap_shape,
            pltpu.VMEM((3, 2 * LANES, rows), f32),
            jax.ShapeDtypeStruct((left_rows, rows), f32),
        ),
        in_specs=[hbm, hbm, vmem, vmem, vmem],
        out_specs=(vmem,) * 11,
        scratch_shapes=[
            pltpu.VMEM((count, columns, rows), f32),
            pltpu.VMEM((count, columns, rows), f32),
            pltpu.VMEM((3, count * T, rows), f32),
            dma((2, CHUNKS)),
        ],
        compiler_params=params,
        cost_estimate=cost(30 * size, 4 * size),
        name="interior",
    )(far(t), far(seed), courant_frac, cell_area, departure_shift)

    from_left, message_left = lax.optimization_barrier((from_left, message_left))
    from_right = lax.ppermute(message_left, "tile", to_left)

    _, ratio, positive, seeds, w, ap, sums = pl.pallas_call(
        left_kernel,
        out_shape=(
            two_strips, whole, wide, whole, w_shape, ap_shape,
            pltpu.VMEM((tile, T, LANES), f32),
        ),
        in_specs=[vmem] * 12,
        out_specs=(vmem,) * 7,
        input_output_aliases={1: 0, 3: 1, 4: 2, 5: 3, 6: 4, 7: 5},
        scratch_shapes=[
            pltpu.VMEM((2, count * T, rows), f32),
            pltpu.VMEM((2, 2 * LANES, rows), f32),
            pltpu.VMEM((2 * T, rows), f32),
            pltpu.VMEM((2 * T, rows), f32),
        ],
        compiler_params=params,
        cost_estimate=cost(10 * size, size),
        name="left_edge",
    )(
        from_left, held(t0), held(s0), held(ratio), held(positive), held(seeds), held(w), held(ap), held(red),
        courant_frac, cell_area, departure_shift,
    )

    x, y, own, positive, sums = pl.pallas_call(
        middle_kernel,
        out_shape=(whole, whole, two_strips, wide, pltpu.VMEM((tile, T, LANES), f32)),
        in_specs=[vmem] * 7,
        out_specs=(vmem,) * 5,
        input_output_aliases={1: 3, 6: 4},
        scratch_shapes=[pltpu.VMEM((bins, columns, rows), f32), pltpu.VMEM((bins, columns, rows), f32)],
        compiler_params=params,
        cost_estimate=cost(30 * size, size),
        name="middle",
    )(held(ratio), held(positive), held(seeds), held(w), held(ap), departure_shift, held(sums))

    sums = lax.all_to_all(sums, "tile", 0, 0)

    tracer_next, tracer_adjoint, _, _ = pl.pallas_call(
        final_kernel,
        out_shape=(
            jax.ShapeDtypeStruct((count, columns, rows), f32),
            jax.ShapeDtypeStruct((count, columns, rows), f32),
            two_strips,
            wide,
        ),
        in_specs=[vmem] * 12,
        out_specs=(hbm, hbm, vmem, vmem),
        input_output_aliases={2: 2, 7: 3},
        scratch_shapes=[
            pltpu.VMEM((3, 2 * LANES, rows), f32),
            pltpu.VMEM((taps, 2 * T, rows), f32),
            pltpu.VMEM((bins, 2 * T, rows), f32),
            pltpu.VMEM((count, columns, rows), f32),
            pltpu.VMEM((count, columns, rows), f32),
            pltpu.VMEM((2 * T, rows), f32),
            pltpu.VMEM((2 * T, rows), f32),
            dma((2, CHUNKS)),
        ],
        compiler_params=params,
        cost_estimate=cost(10 * size, size),
        name="final",
    )(
        sums, from_right, held(t2), held(s2), held(x), held(y), held(own), held(positive), held(w),
        courant_frac, cell_area, departure_shift,
    )
    return tracer_next.reshape(tracer.shape), tracer_adjoint.reshape(tracer.shape)


def solution(mesh):
    return jax.shard_map(
        shards,
        mesh=mesh,
        in_specs=(
            P("group", None, "tile", None),
            P("group", "tile", None),
            P("group", None),
            P("tile", None),
            P("group", None, "tile", None),
        ),
        out_specs=(P("group", None, "tile", None), P("group", None, "tile", None)),
        check_vma=False,
    )
```

time: 42.2 us -> 41 us (0.972)
  blocking collectives: 0 us -> 13.6 us
  starting transfers between devices: 8.78 us -> 0.51 us
  Pallas kernels: 19.1 us -> 14.4 us
  waiting for transfers between devices: 13.3 us -> 11.6 us
    all_to_all x0 -> x1, blocking collectives: none -> 13.6 us  [shards(): sums = lax.all_to_all(sums, 'tile', 0, 0)]
    ppermute x2 -> x1, starting transfers between devices: 4.49 us -> 0.01 us  [shards(): from_right = lax.ppermute(message_left, 'tile', to_left)]
    pallas_call x5 -> x4, Pallas kernels: 17.2 us -> 12.8 us  [the longest x1 4.19 us: shards(): pl.pallas_call(interior_kernel, out_shape=(two_strips, strip, two_strips,...]
    all_to_all x1 -> x0, starting transfers between devices: 3.78 us -> none  [shards(): sums = lax.all_to_all(sums, 'tile', 0, 0)]
    all_to_all x1 -> x0, waiting for transfers between devices: 2.18 us -> none  [shards(): sums = lax.all_to_all(sums, 'tile', 0, 0)]
    ppermute x1, waiting for transfers between devices: 11.1 us -> 11.6 us  [shards(): from_left = lax.ppermute(message, 'tile', to_right)]
  transfers between devices with their start and end apart: 4 -> 2, of which waited for: 2 -> 1; matrix products, arithmetic and copies ran while one was open for 0% -> 0% of each run, Pallas kernels for 30% -> 21%
where the time goes in v3:
time: 41 us; the launch traced here: 40.8 us
  Pallas kernels  14.4 us (35%)
  blocking collectives  13.6 us (33%)
  waiting for transfers between devices  11.6 us (28%)
  between operations  0.68 us (2%)
  starting transfers between devices  0.51 us (1%)
    all_to_all x1, blocking collectives, shards(): sums = lax.all_to_all(sums, 'tile', 0, 0)  13.6 us
    ppermute x1, waiting for transfers between devices, shards(): from_left = lax.ppermute(message, 'tile', to_right)  11.6 us
    pallas_call x1, Pallas kernels, shards(): pl.pallas_call(interior_kernel, out_shape=(two_strips, strip, two_strips,...  4.19 us
    pallas_call x1, Pallas kernels, shards(): pl.pallas_call(final_kernel, out_shape=(jax.ShapeDtypeStruct((count, colu...  4.13 us
    pallas_call x1, Pallas kernels, shards(): pl.pallas_call(middle_kernel, out_shape=(whole, whole, two_strips, wide,...  2.76 us
    pallas_call x1, Pallas kernels, shards(): pl.pallas_call(left_kernel, out_shape=(two_strips, whole, wide, whole, w_...  1.7 us
    pallas_call x1, Pallas kernels, shards(): pl.pallas_call(pack_right_kernel, out_shape=jax.ShapeDtypeStruct((padded(...  1.61 us
  transfers between devices with their start and end apart: 2, of which 1 were waited for; matrix products, arithmetic and copies ran while one was open for 0% of the time, Pallas kernels for 21%

profile of v3, /device:TPU:0, one launch (start us, length us, event | category | flops | bytes accessed | tf_op | source)
XLA Modules:
  0.0 40.8 jit_solution(1412223994937034825)
XLA Ops:
  0.6 0.0 copy-start
  0.6 0.0 copy-start.1
  0.7 0.0 copy-start.2
  0.7 1.6 %pack_right.1 = f32[1752,128]{1,0:T(8,128)S(1)} custom-call(f32[240,24,128]{2,1,0:T(8,128)} %bitcast.4, f32[240,24,128]{2,1,0:T(8,128)} %bitcast.6, f32[16,24,128]{2,1,0:T(8,128)} %f_ref.5, f32[24,128]{1,0:T(8,128)} %area_ref.5, s32[16,128]{1,0:T(8,128)} %n_ref.7), custom_call_target="tpu_custom_call" | custom-call | bytes 2949120 | tf_op jit(solution)/shard_map/pack_right/pallas_call | solution.py:484
  2.3 0.5 %collective-permute-start = (f32[1752,128]{1,0:T(8,128)S(1)}, f32[1752,128]{1,0:T(8,128)S(1)}, u32[]{:S(2)}, u32[]{:S(2)}) collective-permute-start(f32[1752,128]{1,0:T(8,128)S(1)} %pack_right.1), channel_id=1, source_target_pairs={{0,1},{1,2},{2,3},{3,4},{4,5},{5,6},{6,7},{7,8},{8,9},{9,10},{10,1... | collective-permute-start | bytes 2691080 | tf_op jit(solution)/shard_map/ppermute | solution.py:502
  2.8 0.0 copy-done
  2.8 0.0 copy-done.1
  2.8 0.0 copy-done.2
  2.8 4.2 %interior.1 = (f32[240,16,128]{2,1,0:T(8,128)S(1)}, f32[240,8,128]{2,1,0:T(8,128)S(1)}, f32[240,16,128]{2,1,0:T(8,128)S(1)}, f32[240,8,128]{2,1,0:T(8,128)S(1)},...) custom-call(f32[240,24,128]{2,1,0:T(8,128)} %bitcast.5, ...), custom_call_target="tpu_custom_call" | custom-call | flops 88473600 | bytes 11796480 | tf_op jit(solution)/shard_map/interior/pallas_call | solution.py:512
  7.0 11.6 %collective-permute-done.m_ref = f32[1752,128]{1,0:T(8,128)S(1)} collective-permute-done((f32[1752,128]{1,0:T(8,128)S(1)}, f32[1752,128]{1,0:T(8,128)S(1)}, u32[]{:S(2)}, u32[]{:S(2)}) %collective-permute-start) | collective-permute-done | bytes 897056 | tf_op jit(solution)/shard_map/ppermute | solution.py:502
  18.6 0.0 collective-permute-start.1
  18.6 1.7 %left_edge.1 = (f32[240,16,128]{2,1,0:T(8,128)S(1)}, f32[240,24,128]{2,1,0:T(8,128)S(1)}, f32[240,32,128]{2,1,0:T(8,128)S(1)}, f32[240,24,128]{2,1,0:T(8,128)S(1...) custom-call(f32[1752,128]{1,0:T(8,128)S(1)} %collective-permute-done, ...), custom_call_target="tpu_custom_call", output_to_operand_aliasing={{0}: (1, {}), {1}: (3, {}), {2}: (4, {}), {3}: (5, {}), {4}... | custom-call | flops 29491200 | bytes 2949120 | tf_op jit(solution)/shard_map/left_edge/pallas_call | solution.py:535
  20.3 2.8 %middle.1 = (f32[240,24,128]{2,1,0:T(8,128)S(1)}, f32[240,24,128]{2,1,0:T(8,128)S(1)}, f32[240,16,128]{2,1,0:T(8,128)S(1)}, f32[240,32,128]{2,1,0:T(8,128)S(1)}, f32[16,8,128]{2,1,0:T(8,128)S(1)}) custom-call(f32[240,24,128]{2,1,0:T(8,128)S(1)} %get-tuple-element.38.ratio_ref, ...), custom_call_target="tpu_custom_call", output_to_operand_aliasing={{3}: (1, {}), {4}: (6, {})} | custom-call | flops 88473600 | bytes 2949120 | tf_op jit(solution)/shard_map/middle/pallas_call | solution.py:558
  23.1 13.6 %all_to_all.5.g_ref = f32[16,8,128]{2,1,0:T(8,128)S(1)} all-to-all(f32[16,8,128]{2,1,0:T(8,128)S(1)} %get-tuple-element.44), channel_id=1, replica_groups=mesh['group'=2,'tile'=16] {'tile'}, dimensions={0} | all-to-all | bytes 131072 | tf_op jit(solution)/shard_map/all_to_all | solution.py:570
  36.7 0.0 collective-permute-done.1.m_ref
  36.7 4.1 %final.1 = (f32[240,24,128]{2,1,0:T(8,128)}, f32[240,24,128]{2,1,0:T(8,128)}, f32[240,16,128]{2,1,0:T(8,128)S(1)}, f32[240,32,128]{2,1,0:T(8,128)S(1)}) custom-call(f32[16,8,128]{2,1,0:T(8,128)S(1)} %all_to_all.5.g_ref, f32[2496,128]{1,0:T(8,128)S(1)} %collective-permute-done.1.m_ref, ...), custom_call_target="tpu_custom_call", output_to_operand_aliasing={{2}: (2, {}), {3}: (7, {})} | custom-call | flops 29491200 | bytes 2949120 | tf_op jit(solution)/shard_map/final/pallas_call | solution.py:572
Async XLA Ops:
  0.6 2.2 %copy-start = (f32[16,24,128]{2,1,0:T(8,128)S(1)}, f32[16,24,128]{2,1,0:T(8,128)}, u32[]{:S(2)}) copy-start(f32[16,24,128]{2,1,0:T(8,128)} %f_ref.5) | copy-start | bytes 589828
  0.6 2.2 %copy-start.1 = (s32[16,128]{1,0:T(8,128)S(1)}, s32[16,128]{1,0:T(8,128)}, u32[]{:S(2)}) copy-start(s32[16,128]{1,0:T(8,128)} %n_ref.7) | copy-start | bytes 24580
  0.7 2.1 %copy-start.2 = (f32[24,128]{1,0:T(8,128)S(1)}, f32[24,128]{1,0:T(8,128)}, u32[]{:S(2)}) copy-start(f32[24,128]{1,0:T(8,128)} %area_ref.5) | copy-start | bytes 36868
  2.3 16.4 %collective-permute-start = (f32[1752,128]{1,0:T(8,128)S(1)}, f32[1752,128]{1,0:T(8,128)S(1)}, u32[]{:S(2)}, u32[]{:S(2)}) collective-permute-start(f32[1752,128]{1,0:T(8,128)S(1)} %pack_right.1), channel_id=1, source_target_pairs={{0,1},{1,2},{2,3},{3,4},{4,5},{5,6},{6,7},{7,8},{8,9},{9,10},{10,1... | collective-permute-start | bytes 2691080 | tf_op jit(solution)/shard_map/ppermute | solution.py:502
  18.6 18.1 %collective-permute-start.1 = (f32[2496,128]{1,0:T(8,128)S(1)}, f32[2496,128]{1,0:T(8,128)S(1)}, u32[]{:S(2)}, u32[]{:S(2)}) collective-permute-start(f32[2496,128]{1,0:T(8,128)S(1)} %get-tuple-element.45), channel_id=1, source_target_pairs={{1,0},{2,1},{3,2},{4,3},{5,4},{6,5},{7,6},{8,7},{9,8},{10,9},{11,1... | collective-permute-start | bytes 3833864 | tf_op jit(solution)/shard_map/ppermute | solution.py:533

commit v4 on v3

--- a/solution.py
+++ b/solution.py
@@ -13,7 +13,7 @@
 T = 8
 LANES = 128
 VMEM_LIMIT = 20 * 2**20
-CHUNKS = 8
+CHUNKS = 4
 HIGHEST = lax.Precision.HIGHEST
 
 
@@ -373,12 +373,20 @@
     taps = range(LEFT + RIGHT + 1)
     width = 2 * HALO
 
-    def copies_out(c):
+    def copies_out(c, rest):
         span = pl.ds(c * per * bins, per * bins)
+        part = pl.ds(last, T) if rest else pl.ds(0, last)
         return (
-            pltpu.make_async_copy(next_buf.at[span], next_hbm.at[span], out_sems.at[0, c]),
-            pltpu.make_async_copy(adj_buf.at[span], adj_hbm.at[span], out_sems.at[1, c]),
+            pltpu.make_async_copy(next_buf.at[span, part, :], next_hbm.at[span, part, :], out_sems.at[0 + 2 * rest, c]),
+            pltpu.make_async_copy(adj_buf.at[span, part, :], adj_hbm.at[span, part, :], out_sems.at[1 + 2 * rest, c]),
         )
+
+    def leave(rest):
+        def act(c):
+            for copy in copies_out(c - 1, rest):
+                copy.start()
+
+        return act
 
     total = g_ref[0]
     for peer in range(1, peers):
@@ -390,6 +398,20 @@
         for half in range(2):
             column = jnp.broadcast_to(value[half : half + 1], (LANES, LANES)).T
             scale_ref[k, pl.ds(half * LANES, LANES), :] = column
+    def main_body(level, _):
+        for q in range(tiles - 1):
+            part = slice(T * q, T * q + T)
+            area_own = area_ref[part, :]
+            for b in range(bins):
+                lb = level * bins + b
+                rescale = scale_ref[0, pl.ds(lb, 1), :]
+                value = area_own * scale_ref[2, pl.ds(lb, 1), :] + rescale * x_ref[lb, part, :]
+                adj_buf[lb, part, :] = value - scale_ref[1, pl.ds(lb, 1), :] * y_ref[lb, part, :]
+                next_buf[lb, part, :] = own_ref[lb, part, :] * rescale
+        each_chunk(level + 1, per, leave(0))
+        return 0
+
+    lax.fori_loop(0, levels, main_body, 0)
     f_row = count * width
     area_row = f_row + HALO * levels
     area_buf[0:T, :] = area_ref[last:columns, :]
@@ -421,34 +443,24 @@
             seed = jnp.where(near, s2_ref[lb], m_ref[pl.ds(lb * width + HALO, T), :])
             s_buf[b, 0:T, :] = rescale * x_ref[lb, last:columns, :] - feedback * y_ref[lb, last:columns, :]
             s_buf[b, T : 2 * T, :] = (rescale * seed - feedback * area) * ratio
-        for q in range(tiles):
-            part = slice(T * q, T * q + T)
-            area_own = area_ref[part, :]
-            for b in range(bins):
-                lb = level * bins + b
-                rescale = scale_ref[0, pl.ds(lb, 1), :]
-                value = area_own * scale_ref[2, pl.ds(lb, 1), :]
-                if q < tiles - 1:
-                    value = value + rescale * x_ref[lb, part, :] - scale_ref[1, pl.ds(lb, 1), :] * y_ref[lb, part, :]
-                    own = own_ref[lb, part, :]
-                else:
-                    for k in taps:
-                        value = value + weights[k] * s_buf[b, pl.ds(OFF + LEFT - k, T), :]
-                    own = pick_back(lambda r: pos_ref[lb, pl.ds(r, T), :], T * q + OFF, shift_is)
-                adj_buf[lb, part, :] = value
-                next_buf[lb, part, :] = own * rescale
-
-        def leave(c):
-            for copy in copies_out(c - 1):
-                copy.start()
-
-        each_chunk(level + 1, per, leave)
+        part = slice(last, columns)
+        area_own = area_ref[part, :]
+        for b in range(bins):
+            lb = level * bins + b
+            value = area_own * scale_ref[2, pl.ds(lb, 1), :]
+            for k in taps:
+                value = value + weights[k] * s_buf[b, pl.ds(OFF + LEFT - k, T), :]
+            adj_buf[lb, part, :] = value
+            own = pick_back(lambda r: pos_ref[lb, pl.ds(r, T), :], last + OFF, shift_is)
+            next_buf[lb, part, :] = own * scale_ref[0, pl.ds(lb, 1), :]
+        each_chunk(level + 1, per, leave(1))
         return 0
 
     lax.fori_loop(0, levels, level_body, 0)
     for c in range(chunks):
-        for copy in copies_out(c):
-            copy.wait()
+        for rest in range(2):
+            for copy in copies_out(c, rest):
+                copy.wait()
 
 
 def padded(rows):
@@ -588,7 +600,7 @@
             pltpu.VMEM((count, columns, rows), f32),
             pltpu.VMEM((2 * T, rows), f32),
             pltpu.VMEM((2 * T, rows), f32),
-            dma((2, CHUNKS)),
+            dma((4, CHUNKS)),
         ],
         compiler_params=params,
         cost_estimate=cost(10 * size, size),

time: 41 us -> 40.9 us (level)
  transfers between devices with their start and end apart: 2 -> 2, of which waited for: 1 -> 1; matrix products, arithmetic and copies ran while one was open for 0% -> 0% of each run, Pallas kernels for 21% -> 22%
where the time goes in v4:
time: 40.9 us; the launch traced here: 40.7 us
  Pallas kernels  14.4 us (35%)
  blocking collectives  13.6 us (33%)
  waiting for transfers between devices  11.5 us (28%)
  between operations  0.68 us (2%)
  starting transfers between devices  0.51 us (1%)
    all_to_all x1, blocking collectives, shards(): sums = lax.all_to_all(sums, 'tile', 0, 0)  13.6 us
    ppermute x1, waiting for transfers between devices, shards(): from_left = lax.ppermute(message, 'tile', to_right)  11.5 us
    pallas_call x1, Pallas kernels, shards(): pl.pallas_call(interior_kernel, out_shape=(two_strips, strip, two_strips,...  4.35 us
    pallas_call x1, Pallas kernels, shards(): pl.pallas_call(final_kernel, out_shape=(jax.ShapeDtypeStruct((count, colu...  4.01 us
    pallas_call x1, Pallas kernels, shards(): pl.pallas_call(middle_kernel, out_shape=(whole, whole, two_strips, wide,...  2.76 us
    pallas_call x1, Pallas kernels, shards(): pl.pallas_call(left_kernel, out_shape=(two_strips, whole, wide, whole, w_...  1.7 us
    pallas_call x1, Pallas kernels, shards(): pl.pallas_call(pack_right_kernel, out_shape=jax.ShapeDtypeStruct((padded(...  1.61 us
  transfers between devices with their start and end apart: 2, of which 1 were waited for; matrix products, arithmetic and copies ran while one was open for 0% of the time, Pallas kernels for 22%

profile of v4, /device:TPU:0, one launch (start us, length us, event | category | flops | bytes accessed | tf_op | source)
XLA Modules:
  0.0 40.7 jit_solution(14447122393302043074)
XLA Ops:
  0.6 0.0 copy-start
  0.6 0.0 copy-start.1
  0.7 0.0 copy-start.2
  0.7 1.6 %pack_right.1 = f32[1752,128]{1,0:T(8,128)S(1)} custom-call(f32[240,24,128]{2,1,0:T(8,128)} %bitcast.4, f32[240,24,128]{2,1,0:T(8,128)} %bitcast.6, f32[16,24,128]{2,1,0:T(8,128)} %f_ref.5, f32[24,128]{1,0:T(8,128)} %area_ref.5, s32[16,128]{1,0:T(8,128)} %n_ref.7), custom_call_target="tpu_custom_call" | custom-call | bytes 2949120 | tf_op jit(solution)/shard_map/pack_right/pallas_call | solution.py:496
  2.3 0.5 %collective-permute-start = (f32[1752,128]{1,0:T(8,128)S(1)}, f32[1752,128]{1,0:T(8,128)S(1)}, u32[]{:S(2)}, u32[]{:S(2)}) collective-permute-start(f32[1752,128]{1,0:T(8,128)S(1)} %pack_right.1), channel_id=1, source_target_pairs={{0,1},{1,2},{2,3},{3,4},{4,5},{5,6},{6,7},{7,8},{8,9},{9,10},{10,1... | collective-permute-start | bytes 2691080 | tf_op jit(solution)/shard_map/ppermute | solution.py:514
  2.8 0.0 copy-done
  2.8 0.0 copy-done.1
  2.8 0.0 copy-done.2
  2.8 4.4 %interior.1 = (f32[240,16,128]{2,1,0:T(8,128)S(1)}, f32[240,8,128]{2,1,0:T(8,128)S(1)}, f32[240,16,128]{2,1,0:T(8,128)S(1)}, f32[240,8,128]{2,1,0:T(8,128)S(1)},...) custom-call(f32[240,24,128]{2,1,0:T(8,128)} %bitcast.5, ...), custom_call_target="tpu_custom_call" | custom-call | flops 88473600 | bytes 11796480 | tf_op jit(solution)/shard_map/interior/pallas_call | solution.py:524
  7.2 11.5 %collective-permute-done.m_ref = f32[1752,128]{1,0:T(8,128)S(1)} collective-permute-done((f32[1752,128]{1,0:T(8,128)S(1)}, f32[1752,128]{1,0:T(8,128)S(1)}, u32[]{:S(2)}, u32[]{:S(2)}) %collective-permute-start) | collective-permute-done | bytes 897056 | tf_op jit(solution)/shard_map/ppermute | solution.py:514
  18.6 0.0 collective-permute-start.1
  18.6 1.7 %left_edge.1 = (f32[240,16,128]{2,1,0:T(8,128)S(1)}, f32[240,24,128]{2,1,0:T(8,128)S(1)}, f32[240,32,128]{2,1,0:T(8,128)S(1)}, f32[240,24,128]{2,1,0:T(8,128)S(1...) custom-call(f32[1752,128]{1,0:T(8,128)S(1)} %collective-permute-done, ...), custom_call_target="tpu_custom_call", output_to_operand_aliasing={{0}: (1, {}), {1}: (3, {}), {2}: (4, {}), {3}: (5, {}), {4}... | custom-call | flops 29491200 | bytes 2949120 | tf_op jit(solution)/shard_map/left_edge/pallas_call | solution.py:547
  20.3 2.8 %middle.1 = (f32[240,24,128]{2,1,0:T(8,128)S(1)}, f32[240,24,128]{2,1,0:T(8,128)S(1)}, f32[240,16,128]{2,1,0:T(8,128)S(1)}, f32[240,32,128]{2,1,0:T(8,128)S(1)}, f32[16,8,128]{2,1,0:T(8,128)S(1)}) custom-call(f32[240,24,128]{2,1,0:T(8,128)S(1)} %get-tuple-element.38.ratio_ref, ...), custom_call_target="tpu_custom_call", output_to_operand_aliasing={{3}: (1, {}), {4}: (6, {})} | custom-call | flops 88473600 | bytes 2949120 | tf_op jit(solution)/shard_map/middle/pallas_call | solution.py:570
  23.1 13.6 %all_to_all.5.g_ref = f32[16,8,128]{2,1,0:T(8,128)S(1)} all-to-all(f32[16,8,128]{2,1,0:T(8,128)S(1)} %get-tuple-element.44), channel_id=1, replica_groups=mesh['group'=2,'tile'=16] {'tile'}, dimensions={0} | all-to-all | bytes 131072 | tf_op jit(solution)/shard_map/all_to_all | solution.py:582
  36.7 0.0 collective-permute-done.1.m_ref
  36.7 4.0 %final.1 = (f32[240,24,128]{2,1,0:T(8,128)}, f32[240,24,128]{2,1,0:T(8,128)}, f32[240,16,128]{2,1,0:T(8,128)S(1)}, f32[240,32,128]{2,1,0:T(8,128)S(1)}) custom-call(f32[16,8,128]{2,1,0:T(8,128)S(1)} %all_to_all.5.g_ref, f32[2496,128]{1,0:T(8,128)S(1)} %collective-permute-done.1.m_ref, ...), custom_call_target="tpu_custom_call", output_to_operand_aliasing={{2}: (2, {}), {3}: (7, {})} | custom-call | flops 29491200 | bytes 2949120 | tf_op jit(solution)/shard_map/final/pallas_call | solution.py:584
Async XLA Ops:
  0.6 2.2 %copy-start = (f32[16,24,128]{2,1,0:T(8,128)S(1)}, f32[16,24,128]{2,1,0:T(8,128)}, u32[]{:S(2)}) copy-start(f32[16,24,128]{2,1,0:T(8,128)} %f_ref.5) | copy-start | bytes 589828
  0.6 2.2 %copy-start.1 = (s32[16,128]{1,0:T(8,128)S(1)}, s32[16,128]{1,0:T(8,128)}, u32[]{:S(2)}) copy-start(s32[16,128]{1,0:T(8,128)} %n_ref.7) | copy-start | bytes 24580
  0.7 2.1 %copy-start.2 = (f32[24,128]{1,0:T(8,128)S(1)}, f32[24,128]{1,0:T(8,128)}, u32[]{:S(2)}) copy-start(f32[24,128]{1,0:T(8,128)} %area_ref.5) | copy-start | bytes 36868
  2.3 16.4 %collective-permute-start = (f32[1752,128]{1,0:T(8,128)S(1)}, f32[1752,128]{1,0:T(8,128)S(1)}, u32[]{:S(2)}, u32[]{:S(2)}) collective-permute-start(f32[1752,128]{1,0:T(8,128)S(1)} %pack_right.1), channel_id=1, source_target_pairs={{0,1},{1,2},{2,3},{3,4},{4,5},{5,6},{6,7},{7,8},{8,9},{9,10},{10,1... | collective-permute-start | bytes 2691080 | tf_op jit(solution)/shard_map/ppermute | solution.py:514
  18.6 18.1 %collective-permute-start.1 = (f32[2496,128]{1,0:T(8,128)S(1)}, f32[2496,128]{1,0:T(8,128)S(1)}, u32[]{:S(2)}, u32[]{:S(2)}) collective-permute-start(f32[2496,128]{1,0:T(8,128)S(1)} %get-tuple-element.45), channel_id=1, source_target_pairs={{1,0},{2,1},{3,2},{4,3},{5,4},{6,5},{7,6},{8,7},{9,8},{10,9},{11,1... | collective-permute-start | bytes 3833864 | tf_op jit(solution)/shard_map/ppermute | solution.py:545

commit v5 on v4

--- a/solution.py
+++ b/solution.py
@@ -411,7 +411,7 @@
         each_chunk(level + 1, per, leave(0))
         return 0
 
-    lax.fori_loop(0, levels, main_body, 0)
+    lax.fori_loop(0, levels, main_body, 0, unroll=2)
     f_row = count * width
     area_row = f_row + HALO * levels
     area_buf[0:T, :] = area_ref[last:columns, :]

time: 40.9 us -> 40.9 us (level)
  no operation moved by 1% of the time
where the time goes in v5:
time: 40.9 us; the launch traced here: 40.7 us
  Pallas kernels  14.4 us (35%)
  blocking collectives  13.6 us (33%)
  waiting for transfers between devices  11.5 us (28%)
  between operations  0.68 us (2%)
  starting transfers between devices  0.51 us (1%)
    all_to_all x1, blocking collectives, shards(): sums = lax.all_to_all(sums, 'tile', 0, 0)  13.6 us
    ppermute x1, waiting for transfers between devices, shards(): from_left = lax.ppermute(message, 'tile', to_right)  11.5 us
    pallas_call x1, Pallas kernels, shards(): pl.pallas_call(interior_kernel, out_shape=(two_strips, strip, two_strips,...  4.35 us
    pallas_call x1, Pallas kernels, shards(): pl.pallas_call(final_kernel, out_shape=(jax.ShapeDtypeStruct((count, colu...  3.99 us
    pallas_call x1, Pallas kernels, shards(): pl.pallas_call(middle_kernel, out_shape=(whole, whole, two_strips, wide,...  2.76 us
    pallas_call x1, Pallas kernels, shards(): pl.pallas_call(left_kernel, out_shape=(two_strips, whole, wide, whole, w_...  1.7 us
    pallas_call x1, Pallas kernels, shards(): pl.pallas_call(pack_right_kernel, out_shape=jax.ShapeDtypeStruct((padded(...  1.61 us
  transfers between devices with their start and end apart: 2, of which 1 were waited for; matrix products, arithmetic and copies ran while one was open for 0% of the time, Pallas kernels for 22%

profile of v5, /device:TPU:0, one launch (start us, length us, event | category | flops | bytes accessed | tf_op | source)
XLA Modules:
  0.0 40.7 jit_solution(12437520449525238425)
XLA Ops:
  0.6 0.0 copy-start
  0.6 0.0 copy-start.1
  0.7 0.0 copy-start.2
  0.7 1.6 %pack_right.1 = f32[1752,128]{1,0:T(8,128)S(1)} custom-call(f32[240,24,128]{2,1,0:T(8,128)} %bitcast.4, f32[240,24,128]{2,1,0:T(8,128)} %bitcast.6, f32[16,24,128]{2,1,0:T(8,128)} %f_ref.5, f32[24,128]{1,0:T(8,128)} %area_ref.5, s32[16,128]{1,0:T(8,128)} %n_ref.7), custom_call_target="tpu_custom_call" | custom-call | bytes 2949120 | tf_op jit(solution)/shard_map/pack_right/pallas_call | solution.py:496
  2.3 0.5 %collective-permute-start = (f32[1752,128]{1,0:T(8,128)S(1)}, f32[1752,128]{1,0:T(8,128)S(1)}, u32[]{:S(2)}, u32[]{:S(2)}) collective-permute-start(f32[1752,128]{1,0:T(8,128)S(1)} %pack_right.1), channel_id=1, source_target_pairs={{0,1},{1,2},{2,3},{3,4},{4,5},{5,6},{6,7},{7,8},{8,9},{9,10},{10,1... | collective-permute-start | bytes 2691080 | tf_op jit(solution)/shard_map/ppermute | solution.py:514
  2.8 0.0 copy-done
  2.8 0.0 copy-done.1
  2.8 0.0 copy-done.2
  2.8 4.4 %interior.1 = (f32[240,16,128]{2,1,0:T(8,128)S(1)}, f32[240,8,128]{2,1,0:T(8,128)S(1)}, f32[240,16,128]{2,1,0:T(8,128)S(1)}, f32[240,8,128]{2,1,0:T(8,128)S(1)},...) custom-call(f32[240,24,128]{2,1,0:T(8,128)} %bitcast.5, ...), custom_call_target="tpu_custom_call" | custom-call | flops 88473600 | bytes 11796480 | tf_op jit(solution)/shard_map/interior/pallas_call | solution.py:524
  7.2 11.5 %collective-permute-done.m_ref = f32[1752,128]{1,0:T(8,128)S(1)} collective-permute-done((f32[1752,128]{1,0:T(8,128)S(1)}, f32[1752,128]{1,0:T(8,128)S(1)}, u32[]{:S(2)}, u32[]{:S(2)}) %collective-permute-start) | collective-permute-done | bytes 897056 | tf_op jit(solution)/shard_map/ppermute | solution.py:514
  18.6 0.0 collective-permute-start.1
  18.6 1.7 %left_edge.1 = (f32[240,16,128]{2,1,0:T(8,128)S(1)}, f32[240,24,128]{2,1,0:T(8,128)S(1)}, f32[240,32,128]{2,1,0:T(8,128)S(1)}, f32[240,24,128]{2,1,0:T(8,128)S(1...) custom-call(f32[1752,128]{1,0:T(8,128)S(1)} %collective-permute-done, ...), custom_call_target="tpu_custom_call", output_to_operand_aliasing={{0}: (1, {}), {1}: (3, {}), {2}: (4, {}), {3}: (5, {}), {4}... | custom-call | flops 29491200 | bytes 2949120 | tf_op jit(solution)/shard_map/left_edge/pallas_call | solution.py:547
  20.3 2.8 %middle.1 = (f32[240,24,128]{2,1,0:T(8,128)S(1)}, f32[240,24,128]{2,1,0:T(8,128)S(1)}, f32[240,16,128]{2,1,0:T(8,128)S(1)}, f32[240,32,128]{2,1,0:T(8,128)S(1)}, f32[16,8,128]{2,1,0:T(8,128)S(1)}) custom-call(f32[240,24,128]{2,1,0:T(8,128)S(1)} %get-tuple-element.38.ratio_ref, ...), custom_call_target="tpu_custom_call", output_to_operand_aliasing={{3}: (1, {}), {4}: (6, {})} | custom-call | flops 88473600 | bytes 2949120 | tf_op jit(solution)/shard_map/middle/pallas_call | solution.py:570
  23.1 13.6 %all_to_all.5.g_ref = f32[16,8,128]{2,1,0:T(8,128)S(1)} all-to-all(f32[16,8,128]{2,1,0:T(8,128)S(1)} %get-tuple-element.44), channel_id=1, replica_groups=mesh['group'=2,'tile'=16] {'tile'}, dimensions={0} | all-to-all | bytes 131072 | tf_op jit(solution)/shard_map/all_to_all | solution.py:582
  36.7 0.0 collective-permute-done.1.m_ref
  36.7 4.0 %final.1 = (f32[240,24,128]{2,1,0:T(8,128)}, f32[240,24,128]{2,1,0:T(8,128)}, f32[240,16,128]{2,1,0:T(8,128)S(1)}, f32[240,32,128]{2,1,0:T(8,128)S(1)}) custom-call(f32[16,8,128]{2,1,0:T(8,128)S(1)} %all_to_all.5.g_ref, f32[2496,128]{1,0:T(8,128)S(1)} %collective-permute-done.1.m_ref, ...), custom_call_target="tpu_custom_call", output_to_operand_aliasing={{2}: (2, {}), {3}: (7, {})} | custom-call | flops 29491200 | bytes 2949120 | tf_op jit(solution)/shard_map/final/pallas_call | solution.py:584
Async XLA Ops:
  0.6 2.2 %copy-start = (f32[16,24,128]{2,1,0:T(8,128)S(1)}, f32[16,24,128]{2,1,0:T(8,128)}, u32[]{:S(2)}) copy-start(f32[16,24,128]{2,1,0:T(8,128)} %f_ref.5) | copy-start | bytes 589828
  0.6 2.2 %copy-start.1 = (s32[16,128]{1,0:T(8,128)S(1)}, s32[16,128]{1,0:T(8,128)}, u32[]{:S(2)}) copy-start(s32[16,128]{1,0:T(8,128)} %n_ref.7) | copy-start | bytes 24580
  0.7 2.1 %copy-start.2 = (f32[24,128]{1,0:T(8,128)S(1)}, f32[24,128]{1,0:T(8,128)}, u32[]{:S(2)}) copy-start(f32[24,128]{1,0:T(8,128)} %area_ref.5) | copy-start | bytes 36868
  2.3 16.4 %collective-permute-start = (f32[1752,128]{1,0:T(8,128)S(1)}, f32[1752,128]{1,0:T(8,128)S(1)}, u32[]{:S(2)}, u32[]{:S(2)}) collective-permute-start(f32[1752,128]{1,0:T(8,128)S(1)} %pack_right.1), channel_id=1, source_target_pairs={{0,1},{1,2},{2,3},{3,4},{4,5},{5,6},{6,7},{7,8},{8,9},{9,10},{10,1... | collective-permute-start | bytes 2691080 | tf_op jit(solution)/shard_map/ppermute | solution.py:514
  18.6 18.1 %collective-permute-start.1 = (f32[2496,128]{1,0:T(8,128)S(1)}, f32[2496,128]{1,0:T(8,128)S(1)}, u32[]{:S(2)}, u32[]{:S(2)}) collective-permute-start(f32[2496,128]{1,0:T(8,128)S(1)} %get-tuple-element.45), channel_id=1, source_target_pairs={{1,0},{2,1},{3,2},{4,3},{5,4},{6,5},{7,6},{8,7},{9,8},{10,9},{11,1... | collective-permute-start | bytes 3833864 | tf_op jit(solution)/shard_map/ppermute | solution.py:545
